TPU v7x, 512 devices: a whole 4x8x8 slice. The times are simulated.
512 devices in a mesh: seq: 16 (over y_hi, z), res: 32 (over x, y_lo, core).
Axes of the slice: x: 4, y: 8 (y_hi: 2, y_lo: 4; y = y_hi * 4 + y_lo), z: 8, core: 2. Of those that a mesh axis runs over, the one named last changes fastest.
Arguments:
- homolog_matrix: bfloat16 [32, 2048, 256], P('seq', 'res'), may hold values from -6 to 6
- factor_matrix: bfloat16 [256, 64], replicated, may hold values from -0.375 to 0.375
- output_weight: bfloat16 [1024, 128], replicated, may hold values from -1.5 to 1.5
- output_bias: float32 [128], replicated, may hold values from -3 to 3
- pairwise_cotangent: bfloat16 [2048, 2048, 128], P('res', 'seq'), may hold values from -0.19921875 to 0.19921875
Outputs:
- pairwise_update: bfloat16 [2048, 2048, 128], P('res', 'seq')
- alignment_gradient: bfloat16 [32, 2048, 256], P('seq', 'res')
- factor_matrix_deriv: float32 [256, 64], replicated
- output_weight_gradient: float32 [1024, 128], replicated
All inputs are finite; a program needn't handle non-finite values.
Results may differ from a plain program's by a relative error of at most 0.0073.
Values may be sent and summed in bfloat16 or wider, within the bound.
No kernel may reach another device: no remote copies, remote signals or barrier semaphores. Data moves between devices by JAX's collectives and lax.ppermute only.
A program may use at most 64 MiB of HBM per device.

v0:
```python
import jax
import jax.numpy as jnp
from jax import lax
from jax.sharding import PartitionSpec as P


def layer_normalizer(values):
    center = jnp.mean(values, axis=-1, keepdims=True)
    centered = values - center
    variance = jnp.mean(centered * centered, axis=-1, keepdims=True)
    reciprocal_count = lax.rsqrt(variance + 1e-05)
    return (centered * reciprocal_count, reciprocal_count)


def body(homolog_matrix, factor_matrix, output_weight, output_bias, pairwise_cotangent):
    sequence_shard, residue_shard, channel_count = homolog_matrix.shape
    half = factor_matrix.shape[1] // 2
    pair_channels = output_weight.shape[1]
    normalized_alignment, reciprocal_count = layer_normalizer(homolog_matrix.astype(jnp.float32))
    standardized_reduced = normalized_alignment.astype(jnp.bfloat16)
    mapped_features = jnp.einsum(
        "src,ck->srk", standardized_reduced, factor_matrix, preferred_element_type=jnp.float32
    )
    left_proj = mapped_features[:, :, :half].astype(jnp.bfloat16)
    right_proj = mapped_features[:, :, half:].astype(jnp.bfloat16)
    rows_left = lax.all_gather(left_proj, "seq", axis=0, tiled=True)
    spread = lax.all_gather(right_proj, "res", axis=1, tiled=True)
    cols_right = lax.all_to_all(spread, "seq", split_axis=1, concat_axis=0, tiled=True)
    total_seq = rows_left.shape[0]
    col_count = cols_right.shape[1]
    inv_count = 1.0 / total_seq
    rows_per = min(8, residue_shard)
    block_count = residue_shard // rows_per

    def tile_step(totals, block_idx):
        wo_total, right_total = totals
        start = block_idx * rows_per
        left_block = lax.dynamic_slice_in_dim(rows_left, start, rows_per, 1)
        cot_block = lax.dynamic_slice_in_dim(pairwise_cotangent, start, rows_per, 0).reshape(
            -1, pair_channels
        )
        outer_sum = (
            jnp.einsum("sic,sjd->ijcd", left_block, cols_right, preferred_element_type=jnp.float32)
            * inv_count
        )
        outer_low = outer_sum.reshape(-1, half * half).astype(jnp.bfloat16)
        pair_block = (
            jnp.dot(outer_low, output_weight, preferred_element_type=jnp.float32) + output_bias
        )
        pair_block = pair_block.astype(jnp.bfloat16).reshape(rows_per, col_count, pair_channels)
        grad_outer = jnp.einsum(
            "pe,fe->pf", cot_block, output_weight, preferred_element_type=jnp.float32
        ).astype(jnp.bfloat16)
        wo_total = wo_total + jnp.einsum(
            "pf,pe->fe", outer_low, cot_block, preferred_element_type=jnp.float32
        )
        grad_tile = grad_outer.reshape(rows_per, col_count, half, half)
        left_terms = (
            jnp.einsum("ijcd,sjd->sic", grad_tile, cols_right, preferred_element_type=jnp.float32)
            * inv_count
        )
        right_total = (
            right_total
            + jnp.einsum("ijcd,sic->sjd", grad_tile, left_block, preferred_element_type=jnp.float32)
            * inv_count
        )
        return ((wo_total, right_total), (pair_block, left_terms))

    start_totals = (
        jnp.zeros((half * half, pair_channels), jnp.float32),
        jnp.zeros((total_seq, col_count, half), jnp.float32),
    )
    totals, stacked = lax.scan(tile_step, start_totals, jnp.arange(block_count, dtype=jnp.int32))
    wo_partial, right_partial = totals
    pair_blocks, left_blocks = stacked
    pairwise_update = pair_blocks.reshape(residue_shard, col_count, pair_channels)
    left_partial = jnp.moveaxis(left_blocks, 0, 1).reshape(total_seq, residue_shard, half)
    left_grad = lax.psum_scatter(left_partial, "seq", scatter_dimension=0, tiled=True)
    moved = lax.all_to_all(
        lax.all_to_all(right_partial[None], "seq", split_axis=1, concat_axis=2, tiled=True),
        "res",
        split_axis=2,
        concat_axis=0,
        tiled=True,
    )
    right_grad = jnp.sum(moved, axis=0)
    both_grads = jnp.concatenate([left_grad, right_grad], axis=-1).astype(jnp.bfloat16)
    proj_partial = jnp.einsum(
        "src,srk->ck", standardized_reduced, both_grads, preferred_element_type=jnp.float32
    )
    factor_matrix_deriv, output_weight_gradient = lax.psum(
        (proj_partial, wo_partial), ("seq", "res")
    )
    standardized_deriv = jnp.einsum(
        "srk,ck->src", both_grads, factor_matrix, preferred_element_type=jnp.float32
    )
    averaged_gradient = jnp.mean(standardized_deriv, axis=-1, keepdims=True)
    averaged_outer = jnp.mean(standardized_deriv * normalized_alignment, axis=-1, keepdims=True)
    alignment_gradient = (
        reciprocal_count
        * (standardized_deriv - averaged_gradient - normalized_alignment * averaged_outer)
    ).astype(jnp.bfloat16)
    return (pairwise_update, alignment_gradient, factor_matrix_deriv, output_weight_gradient)


def solution(mesh):
    placed = (P("seq", "res", None), P(), P(), P(), P("res", "seq", None))
    return jax.shard_map(
        body,
        mesh=mesh,
        in_specs=placed,
        out_specs=(P("res", "seq", None), P("seq", "res", None), P(), P()),
        check_vma=False,
    )
```

profile of v0, /device:TPU:1, one launch (start us, length us, event | category | flops | bytes accessed | tf_op | source)
XLA Modules:
  0.0 789.5 jit_solution(14470489879476738789)
XLA Ops:
  10.4 50.0 %all_gather.7 = bf16[2,2048,32]{2,0,1:T(2,128)(2,1)S(1)} all-gather(bf16[2,64,32]{2,0,1:T(2,128)(2,1)S(1)} %copy.94), channel_id=1, replica_groups=mesh['seq'=16,'res'=32] {'res'}, dimensions={1}, use_global_device_ids=true | all-gather | bytes 270336 | tf_op jit(solution)/shard_map/all_gather | solution.py:27
  60.3 1.7 reshape.60
  62.0 12.5 %all-to-all-start = ((bf16[16,2,4096]{2,1,0:T(2,128)(2,1)}), bf16[16,2,4096]{2,1,0:T(2,128)(2,1)S(1)}, u32[]{:S(2)}, u32[]{:S(2)}) async-start(bf16[16,2,4096]{2,1,0:T(2,128)(2,1)} %reshape.60), calls=%async_computation | async-start | bytes 524288 | tf_op jit(solution)/shard_map/all_to_all | solution.py:28
  74.6 47.3 %all_gather.6 = bf16[32,64,32]{1,2,0:T(8,128)(2,1)S(1)} all-gather(bf16[2,64,32]{1,2,0:T(8,128)(2,1)S(1)} %get-tuple-element.219), channel_id=1, replica_groups=mesh['seq'=16,'res'=32] {'seq'}, dimensions={0}, use_global_device_ids=true | all-gather | bytes 139264 | tf_op jit(solution)/shard_map/all_gather | solution.py:26
  121.9 1.6 copy.96
  124.8 132.5 %while.17 = (s32[]{:T(128)}, f32[1024,128]{1,0:T(8,128)}, f32[32,128,32]{1,0,2:T(8,128)S(1)}, bf16[8,8,128,128]{3,2,1,0:T(8,128)(2,1)}, f32[8,32,8,32]{1,2,3,0:T...) while((s32[]{:T(128)}, f32[1024,128]{1,0:T(8,128)}, ...), condition=%wide.region_3.4_spmd.clone, body=%wide.region_2.3_spmd.clone.sunk | while | flops 1010704384 | bytes 34603812 | solution.py:73
  127.0 2.1 convolution_convert_fusion.3
  129.1 2.9 copy.148
  132.6 2.2 fusion.93
  136.1 1.5 fusion.91
  143.6 2.1 convolution_convert_fusion.3
  145.7 2.9 copy.148
  149.1 2.2 fusion.93
  152.7 1.5 fusion.91
  154.2 1.4 copy.147
  160.2 2.1 convolution_convert_fusion.3
  162.2 2.9 copy.148
  165.7 2.2 fusion.93
  169.2 1.5 fusion.91
  176.7 2.1 convolution_convert_fusion.3
  178.8 2.9 copy.148
  182.2 2.2 fusion.93
  185.8 1.5 fusion.91
  193.3 2.1 convolution_convert_fusion.3
  195.3 2.9 copy.148
  198.8 2.2 fusion.93
  202.3 1.5 fusion.91
  209.8 2.1 convolution_convert_fusion.3
  211.9 2.9 copy.148
  215.3 2.2 fusion.93
  218.9 1.5 fusion.91
  226.4 2.1 convolution_convert_fusion.3
  228.4 2.9 copy.148
  231.9 2.2 fusion.93
  235.4 1.5 fusion.91
  242.9 2.1 convolution_convert_fusion.3
  245.0 2.9 copy.148
  248.5 2.2 fusion.93
  252.0 1.5 fusion.91
  257.6 15.7 %all_to_all.48 = f32[1,32,128,32]{2,3,0,1:T(8,128)S(1)} all-to-all(f32[1,32,128,32]{2,3,0,1:T(8,128)S(1)} %bitcast.150), channel_id=1, replica_groups=mesh['seq'=16,'res'=32] {'seq'}, dimensions={1} | all-to-all | bytes 1048576 | tf_op jit(solution)/shard_map/all_to_all | solution.py:80
  274.7 2.8 reshape.62
  277.6 12.3 %all-to-all-start.2 = ((f32[32,1,4096]{2,1,0:T(1,128)}), f32[32,1,4096]{2,1,0:T(1,128)S(1)}, u32[]{:S(2)}, u32[]{:S(2)}) async-start(f32[32,1,4096]{2,1,0:T(1,128)} %reshape.62), calls=%async_computation.3 | async-start | bytes 1048576 | tf_op jit(solution)/shard_map/all_to_all | solution.py:79
  292.1 208.9 %reduce-scatter.2.cloned.1.call-done = f32[2,64,32]{1,2,0:T(8,128)} async-done(((f32[32,64,32]{1,2,0:T(8,128)}), f32[2,64,32]{1,2,0:T(8,128)}) %reduce-scatter.2.cloned.1.call-update) | async-done | bytes 16400 | tf_op jit(solution)/shard_map/reduce_scatter | solution.py:78
  502.3 1.9 reduce.3
  504.3 1.8 reshape.63
  509.2 270.1 %all-reduce.3.cloned.1.call-done = (f32[256,64]{0,1:T(8,128)}, f32[1024,128]{1,0:T(8,128)}) async-done(((f32[256,64]{0,1:T(8,128)}, f32[1024,128]{1,0:T(8,128)}), (f32[256,64]{0,1:T(8,128)}, f32[1024,128]{1,0:T(8,128)})) %all-reduce.3.cloned.1.call-update) | async-done | bytes 589840 | tf_op jit(solution)/shard_map/psum | solution.py:91
  779.3 1.5 copy.169
  780.7 1.9 copy.170
  (138 shorter events, 69.1 us)
Async XLA Ops:
  7.2 2.0 copy-start
  62.0 62.8 %copy-start.1 = (bf16[1024,128]{1,0:T(8,128)(2,1)S(1)}, bf16[1024,128]{1,0:T(8,128)(2,1)}, u32[]{:S(2)}) copy-start(bf16[1024,128]{1,0:T(8,128)(2,1)} %param.9) | copy-start | bytes 786436
  62.0 62.8 %copy-start.6 = (f32[128]{0:T(128)S(1)}, f32[128]{0:T(128)}, u32[]{:S(2)}) copy-start(f32[128]{0:T(128)} %param.10) | copy-start | bytes 1540
  62.0 61.5 %all-to-all-start = ((bf16[16,2,4096]{2,1,0:T(2,128)(2,1)}), bf16[16,2,4096]{2,1,0:T(2,128)(2,1)S(1)}, u32[]{:S(2)}, u32[]{:S(2)}) async-start(bf16[16,2,4096]{2,1,0:T(2,128)(2,1)} %reshape.60), calls=%async_computation | async-start | bytes 524288 | tf_op jit(solution)/shard_map/all_to_all | solution.py:28
  137.6 1.4 copy-start.4
  139.9 0.8 copy-start.5
  154.2 1.4 copy-start.4
  156.4 0.8 copy-start.5
  170.7 1.4 copy-start.4
  173.0 0.8 copy-start.5
  187.3 1.4 copy-start.4
  189.5 0.8 copy-start.5
  203.8 1.4 copy-start.4
  206.1 0.8 copy-start.5
  220.4 1.4 copy-start.4
  222.6 0.8 copy-start.5
  237.0 1.4 copy-start.4
  239.2 0.8 copy-start.5
  253.5 1.4 copy-start.4
  255.7 0.8 copy-start.5
  274.7 15.2 %copy-start.2 = (f32[8,32,8,32]{1,2,3,0:T(8,128)S(1)}, f32[8,32,8,32]{1,2,3,0:T(8,128)}, u32[]{:S(2)}) copy-start(f32[8,32,8,32]{1,2,3,0:T(8,128)} %get-tuple-element.65) | copy-start | bytes 786436
  277.6 224.3 %all-to-all-start.2 = ((f32[32,1,4096]{2,1,0:T(1,128)}), f32[32,1,4096]{2,1,0:T(1,128)S(1)}, u32[]{:S(2)}, u32[]{:S(2)}) async-start(f32[32,1,4096]{2,1,0:T(1,128)} %reshape.62), calls=%async_computation.3 | async-start | bytes 1048576 | tf_op jit(solution)/shard_map/all_to_all | solution.py:79
  289.9 211.2 %reduce-scatter.2.cloned.1.call-start = ((), (), s32[]{:S(2)}) async-start(), calls=%async_computation.4 | async-start | bytes 557056 | tf_op jit(solution)/shard_map/reduce_scatter | solution.py:78
  292.1 487.2 %all-reduce.3.cloned.1.call-start = ((), (), s32[]{:S(2)}) async-start(), calls=%async_computation.5 | async-start | bytes 1179648 | tf_op jit(solution)/shard_map/psum | solution.py:91
  504.2 3.0 copy-start.3
Sparse Core Ops, SparseCore 0:
  295.1 205.8 reduce-scatter.1
  508.5 270.7 all-reduce.2
where the time goes:
time: 792 us; the launch traced here: 789 us
  waiting for transfers between devices  479 us (60%)
  blocking collectives  113 us (14%)
  local copies, waits for them, and re-layouts  74 us (9%)
  matrix products  71.7 us (9%)
  starting transfers between devices  24.9 us (3%)
  between operations  14.3 us (2%)
    psum x1, waiting for transfers between devices, body(): lax.psum((proj_partial, wo_partial), ('seq', 'res'))  270 us
    reduce_scatter x1, waiting for transfers between devices, body(): lax.psum_scatter(left_partial, 'seq', scatter_dimension=0, tiled=True)  209 us
    all_gather x1, blocking collectives, body(): spread = lax.all_gather(right_proj, 'res', axis=1, tiled=True)  50 us
    all_gather x1, blocking collectives, body(): rows_left = lax.all_gather(left_proj, 'seq', axis=0, tiled=True)  47.3 us
    convert_element_type x8, local copies, waits for them, and re-layouts, tile_step(): grad_outer = jnp.einsum('pe,fe->pf', cot_block, output_weight, preferred_...  22.8 us
    dot_general x8, matrix products, tile_step(): jnp.einsum('ijcd,sic->sjd', grad_tile, left_block, preferred_element_type...  17.4 us
    dot_general x8, matrix products, tile_step(): jnp.einsum('pe,fe->pf', cot_block, output_weight, preferred_element_type=...  16.5 us
  transfers between devices with their start and end apart: 4, of which 2 were waited for; matrix products, arithmetic and copies ran while one was open for 1% of the time, Pallas kernels for 0%

commit v1 on v0

v1 whole, which is shorter than its diff:
```python
import functools

import jax
import jax.numpy as jnp
from jax import lax
from jax.experimental import pallas as pl
from jax.experimental.pallas import tpu as pltpu
from jax.sharding import PartitionSpec as P

BF = jnp.bfloat16
F32 = jnp.float32
LANES = 128
VMEM_BYTES = 48 * 1024 * 1024
NN = (((1,), (0,)), ((), ()))
NT = (((1,), (1,)), ((), ()))


def dot(a, b, dims=NN):
    return lax.dot_general(a, b, dims, preferred_element_type=F32)


def params():
    return pltpu.CompilerParams(vmem_limit_bytes=VMEM_BYTES)


def whole(shape):
    return pl.BlockSpec(shape, lambda *_: (0,) * len(shape))


def low_lanes(shape, width):
    return lax.broadcasted_iota(jnp.int32, shape, len(shape) - 1) < width


def wide_cotangent(cot_ref):
    return jnp.concatenate([cot_ref[i] for i in range(cot_ref.shape[0])], axis=1)


def left_rows_kernel(recv_ref, spread, rows_ref, inv_count):
    nq, width, lanes = recv_ref.shape
    per = lanes // width
    residues = lanes // 2
    for high in range(nq // per):
        block = recv_ref[high * per : (high + 1) * per].reshape(lanes, lanes).astype(F32)
        turned = block.T * inv_count
        for low in range(per):
            shift = (lanes - low * width) % lanes
            part = turned if shift == 0 else pltpu.roll(turned, shift, 1)
            spread[pl.ds((high * per + low) * lanes, lanes), :] = part

    def one(i, carry):
        for s in range(2):
            part = spread[pl.ds(s * residues + i, nq, stride=lanes), :].astype(BF)
            rows_ref[pl.ds(pl.multiple_of((i * 2 + s) * nq, nq), nq), :] = part
        return carry

    lax.fori_loop(0, residues, one, 0, unroll=8)


def first_kernel(inv_count, recv_ref, w_ref, cot_ref, q_ref, rows_ref, out_ref, spread, acc):
    step = pl.program_id(0)
    block = cot_ref.shape[0]
    nq, width, lanes = recv_ref.shape
    seqs = 2 * nq

    @pl.when(step == 0)
    def _():
        left_rows_kernel(recv_ref, spread, rows_ref, inv_count)

    rows = rows_ref[pl.ds(pl.multiple_of(step * block * seqs, block * seqs), block * seqs), :][:, :width]
    pair = 2 * lanes
    for n in range(w_ref.shape[1] // pair):
        piece = dot(rows, w_ref[:, n * pair : (n + 1) * pair]).astype(BF)
        for k in range(2):
            d = n * 2 + k
            for i in range(block):
                q_ref[0, d * seqs : (d + 1) * seqs, i * lanes : (i + 1) * lanes] = piece[
                    i * seqs : (i + 1) * seqs, k * lanes : (k + 1) * lanes
                ]
    cot = wide_cotangent(cot_ref)
    part = dot(q_ref[0], cot, NT)

    @pl.when(step == 0)
    def _():
        acc[...] = part

    @pl.when(step > 0)
    def _():
        acc[...] += part

    @pl.when(step == pl.num_programs(0) - 1)
    def _():
        low = low_lanes((width, lanes), lanes // 2)
        for q in range(nq):
            a = acc[pl.ds(q, width, stride=seqs), :]
            b = acc[pl.ds(nq + q, width, stride=seqs), :]
            out_ref[2 * q] = jnp.where(low, a, pltpu.roll(b, lanes // 2, 1)).astype(BF)
            out_ref[2 * q + 1] = jnp.where(low, pltpu.roll(a, lanes // 2, 1), b).astype(BF)


def first(recv, w, cot, inv_count, block=8):
    nq, width, lanes = recv.shape
    residues, cols, ch = cot.shape
    seqs = 2 * nq
    steps = residues // block
    return pl.pallas_call(
        functools.partial(first_kernel, inv_count),
        grid=(steps,),
        in_specs=[
            whole(recv.shape),
            whole(w.shape),
            pl.BlockSpec((block, cols, ch), lambda s: (s, 0, 0)),
        ],
        out_specs=[
            pl.BlockSpec((1, width * seqs, block * ch), lambda s: (s, 0, 0)),
            whole((residues * seqs, lanes)),
            whole((2 * nq, width, lanes)),
        ],
        out_shape=[
            jax.ShapeDtypeStruct((steps, width * seqs, block * ch), BF),
            jax.ShapeDtypeStruct((residues * seqs, lanes), BF),
            jax.ShapeDtypeStruct((2 * nq, width, lanes), BF),
        ],
        scratch_shapes=[
            pltpu.VMEM((nq * lanes, lanes), F32),
            pltpu.VMEM((width * seqs, cols), F32),
        ],
        compiler_params=params(),
        cost_estimate=pl.CostEstimate(flops=40_000_000_000, bytes_accessed=20_000_000, transcendentals=0),
        name="first",
    )(recv, w, cot)


def second_kernel(inv_count, recv_ref, w_ref, cot_ref, h_ref, rt_ref, out_ref, spread, left):
    step = pl.program_id(0)
    block = cot_ref.shape[0]
    nr, width, lanes = recv_ref.shape
    nq = nr // 2
    seqs = 2 * nq
    residues = left.shape[0] // seqs

    @pl.when(step == 0)
    def _():
        spread[...] = recv_ref[...].reshape(nr * width, lanes).astype(F32)
        low = low_lanes((nq, lanes), lanes // 2)
        for d in range(width):
            a = spread[pl.ds(d, nq, stride=2 * width), :]
            b = spread[pl.ds(width + d, nq, stride=2 * width), :]
            rt_ref[(2 * d) * nq : (2 * d + 1) * nq, :] = jnp.where(low, a, pltpu.roll(b, lanes // 2, 1)).astype(BF)
            rt_ref[(2 * d + 1) * nq : (2 * d + 2) * nq, :] = jnp.where(low, pltpu.roll(a, lanes // 2, 1), b).astype(BF)

    cot = wide_cotangent(cot_ref)
    group = 8
    for m in range(width // group):
        mine = rt_ref[m * group * seqs : (m + 1) * group * seqs, :]
        for n in range(block // 2):
            piece = dot(mine, cot[:, n * 2 * lanes : (n + 1) * 2 * lanes]).astype(BF)
            for g in range(group):
                d = m * group + g
                for k in range(2):
                    i = 2 * n + k
                    h_ref[i * seqs : (i + 1) * seqs, d * lanes : (d + 1) * lanes] = piece[
                        g * seqs : (g + 1) * seqs, k * lanes : (k + 1) * lanes
                    ]
    start = pl.multiple_of(step * block * seqs, block * seqs)
    left[pl.ds(start, block * seqs), :width] = dot(h_ref[...], w_ref[...], NT) * inv_count

    @pl.when(step == pl.num_programs(0) - 1)
    def _():
        per = lanes // width
        lane = lax.broadcasted_iota(jnp.int32, (lanes, lanes), 1)
        for high in range(nq // per):
            total = None
            for low in range(per):
                q = high * per + low
                part = jnp.concatenate(
                    [left[pl.ds(s * nq + q, residues, stride=seqs), :] for s in range(2)], axis=0
                )
                if low == 0:
                    total = part
                else:
                    total = jnp.where(lane < low * width, total, pltpu.roll(part, low * width, 1))
            out_ref[high * per : (high + 1) * per] = total.T.astype(BF).reshape(per, width, lanes)


def second(recv, w, cot, inv_count, block=8):
    nr, width, lanes = recv.shape
    residues, cols, ch = cot.shape
    nq = nr // 2
    seqs = 2 * nq
    steps = residues // block
    return pl.pallas_call(
        functools.partial(second_kernel, inv_count),
        grid=(steps,),
        in_specs=[
            whole(recv.shape),
            whole(w.shape),
            pl.BlockSpec((block, cols, ch), lambda s: (s, 0, 0)),
        ],
        out_specs=[
            pl.BlockSpec((block * seqs, width * ch), lambda s: (s, 0)),
            whole((width * seqs, cols)),
            whole((nq, width, lanes)),
        ],
        out_shape=[
            jax.ShapeDtypeStruct((residues * seqs, width * ch), BF),
            jax.ShapeDtypeStruct((width * seqs, cols), BF),
            jax.ShapeDtypeStruct((nq, width, lanes), BF),
        ],
        scratch_shapes=[
            pltpu.VMEM((nr * width, lanes), F32),
            pltpu.VMEM((residues * seqs, lanes), F32),
        ],
        compiler_params=params(),
        cost_estimate=pl.CostEstimate(flops=40_000_000_000, bytes_accessed=20_000_000, transcendentals=0),
        name="second",
    )(recv, w, cot)


def third_kernel(rows_ref, h_ref, out_ref, turned):
    @pl.when(pl.program_id(0) == 0)
    def _():
        rows = rows_ref.shape[0]
        for k in range(rows // LANES):
            part = rows_ref[k * LANES : (k + 1) * LANES, :].astype(F32).T
            turned[:, k * LANES : (k + 1) * LANES] = part[: turned.shape[0]].astype(BF)

    total = dot(turned[...], h_ref[...])
    for d in range(out_ref.shape[0]):
        out_ref[d] = total[:, d * LANES : (d + 1) * LANES].astype(BF)


def third(rows, h, width, block=1024):
    count, wide = h.shape
    return pl.pallas_call(
        third_kernel,
        grid=(wide // block,),
        in_specs=[whole(rows.shape), pl.BlockSpec((count, block), lambda s: (0, s))],
        out_specs=pl.BlockSpec((block // LANES, width, LANES), lambda s: (s, 0, 0)),
        out_shape=jax.ShapeDtypeStruct((wide // LANES, width, LANES), BF),
        scratch_shapes=[pltpu.VMEM((width, count), BF)],
        compiler_params=params(),
        cost_estimate=pl.CostEstimate(flops=20_000_000_000, bytes_accessed=17_000_000, transcendentals=0),
        name="third",
    )(rows, h)


def fourth_kernel(rt_ref, q_ref, bias_ref, out_ref, r):
    @pl.when(pl.program_id(0) == 0)
    def _():
        for k in range(rt_ref.shape[0] // LANES):
            r[:, k * LANES : (k + 1) * LANES] = rt_ref[k * LANES : (k + 1) * LANES, :].astype(F32).T.astype(BF)

    bias = bias_ref[...]
    mine = r[...]
    for n in range(out_ref.shape[0] // 2):
        piece = dot(mine, q_ref[0, :, n * 2 * LANES : (n + 1) * 2 * LANES])
        for k in range(2):
            out_ref[2 * n + k] = (piece[:, k * LANES : (k + 1) * LANES] + bias).astype(BF)


def fourth(rt, q, bias):
    steps, depth, wide = q.shape
    cols = rt.shape[1]
    ch = bias.shape[1]
    block = wide // ch
    return pl.pallas_call(
        fourth_kernel,
        grid=(steps,),
        in_specs=[whole(rt.shape), pl.BlockSpec((1, depth, wide), lambda s: (s, 0, 0)), whole(bias.shape)],
        out_specs=pl.BlockSpec((block, cols, ch), lambda s: (s, 0, 0)),
        out_shape=jax.ShapeDtypeStruct((steps * block, cols, ch), BF),
        scratch_shapes=[pltpu.VMEM((cols, depth), BF)],
        compiler_params=params(),
        cost_estimate=pl.CostEstimate(flops=20_000_000_000, bytes_accessed=19_000_000, transcendentals=0),
        name="fourth",
    )(rt, q, bias)


def before_kernel(x_ref, factor_ref, left_ref, right_ref):
    low_normed = standardize(x_ref)[0].astype(BF)
    mapped = dot(low_normed, factor_ref[...])
    width = mapped.shape[1] // 2
    padded = jnp.concatenate([mapped, jnp.zeros((mapped.shape[0], LANES - 2 * width), F32)], axis=1)
    turned = padded.T.astype(BF)
    for q in range(left_ref.shape[0]):
        left_ref[q] = turned[:width]
    right_ref[...] = turned[width : 2 * width]


def standardize(x_ref):
    seqs, residues, ch = x_ref.shape
    x = x_ref[...].reshape(seqs * residues, ch).astype(F32)
    centered = x - jnp.mean(x, axis=-1, keepdims=True)
    variance = jnp.mean(centered * centered, axis=-1, keepdims=True)
    scale = lax.rsqrt(variance + 1e-05)
    return centered * scale, scale


def before(x, factor, copies):
    width = factor.shape[1] // 2
    rows = x.shape[0] * x.shape[1]
    return pl.pallas_call(
        before_kernel,
        out_shape=[
            jax.ShapeDtypeStruct((copies, width, rows), BF),
            jax.ShapeDtypeStruct((width, rows), BF),
        ],
        compiler_params=params(),
        name="before",
    )(x, factor)


def after_kernel(left_ref, right_ref, x_ref, factor_ref, wo_ref, grad_ref, out_ref):
    left = jnp.sum(left_ref[...].astype(F32), axis=0)
    both = jnp.concatenate([left, right_ref[...]], axis=0)
    rows = both.shape[1]
    low_both = both.astype(BF)
    normed, scale = standardize(x_ref)
    factor_part = dot(low_both, normed.astype(BF))
    padded = jnp.concatenate([both, jnp.zeros((LANES - both.shape[0], rows), F32)], axis=0)
    turned = padded.T[:, : both.shape[0]].astype(BF)
    deriv = dot(turned, factor_ref[...], NT)
    mean = jnp.mean(deriv, axis=-1, keepdims=True)
    along = jnp.mean(deriv * normed, axis=-1, keepdims=True)
    grad_ref[...] = (scale * (deriv - mean - normed * along)).astype(BF).reshape(grad_ref.shape)
    chunks, width, _ = wo_ref.shape
    extra = out_ref.shape[1] - width
    out_ref[:, :width, :] = wo_ref[...]
    out_ref[:, width:, :] = jnp.zeros((chunks, extra, LANES), BF)
    stacked = jnp.concatenate(
        [factor_part[:, k * LANES : (k + 1) * LANES] for k in range(factor_part.shape[1] // LANES)], axis=0
    ).astype(BF)
    for k in range(stacked.shape[0] // extra):
        out_ref[k, width:, :] = stacked[k * extra : (k + 1) * extra]


def after(left, right, x, factor, wo):
    chunks, width, lanes = wo.shape
    return pl.pallas_call(
        after_kernel,
        out_shape=[
            jax.ShapeDtypeStruct(x.shape, BF),
            jax.ShapeDtypeStruct((chunks, width + 16, lanes), BF),
        ],
        compiler_params=params(),
        name="after",
    )(left, right, x, factor, wo)


def total_kernel(in_ref, out_ref):
    out_ref[...] = jnp.sum(in_ref[...].astype(F32), axis=0)


def total(parts):
    return pl.pallas_call(
        total_kernel,
        out_shape=jax.ShapeDtypeStruct(parts.shape[1:], F32),
        compiler_params=params(),
        name="total",
    )(parts)


def total_copies_kernel(in_ref, out_ref):
    summed = jnp.sum(in_ref[...].astype(F32), axis=0).astype(BF)
    for k in range(out_ref.shape[0]):
        out_ref[k] = summed


def total_copies(parts, copies):
    return pl.pallas_call(
        total_copies_kernel,
        out_shape=jax.ShapeDtypeStruct((copies,) + parts.shape[1:], BF),
        compiler_params=params(),
        name="total_copies",
    )(parts)


def last_kernel(in_ref, factor_ref, weight_ref):
    chunks, tall, lanes = in_ref.shape
    extra = 16
    width = tall - extra
    for d in range(chunks):
        weight_ref[pl.ds(d, width, stride=chunks), :] = in_ref[d, :width, :].astype(F32)
    ch, both = factor_ref.shape
    used = ch * both // (lanes * extra)
    stacked = in_ref[:used, width:, :].reshape(used * extra, lanes).astype(F32)
    halves = ch // lanes
    for k in range(halves):
        part = stacked[k * both : (k + 1) * both]
        padded = jnp.concatenate([part, jnp.zeros((lanes - both, lanes), F32)], axis=0)
        factor_ref[k * lanes : (k + 1) * lanes, :] = padded.T[:, :both]


def last(parts, factor_shape):
    chunks, tall, lanes = parts.shape
    return pl.pallas_call(
        last_kernel,
        out_shape=[
            jax.ShapeDtypeStruct(factor_shape, F32),
            jax.ShapeDtypeStruct((chunks * (tall - 16), lanes), F32),
        ],
        compiler_params=params(),
        name="last",
    )(parts)


def exchange(parts, axis):
    return lax.all_to_all(parts, axis, 0, 0, tiled=True)


def body(nq, nr, homolog_matrix, factor_matrix, output_weight, output_bias, pairwise_cotangent):
    width = factor_matrix.shape[1] // 2
    inv_count = 1.0 / (2 * nq)
    there = [(s * nr + r, (r // 2) * nr + 2 * s + r % 2) for s in range(nq) for r in range(nr)]
    back = [(b, a) for a, b in there]
    w = output_weight.reshape(width, -1)
    bias = output_bias.reshape(1, -1)
    left_parts, right_mine = before(homolog_matrix, factor_matrix, nq)
    right_moved = lax.ppermute(right_mine, ("seq", "res"), there)
    left_all = exchange(left_parts, "seq")
    right_all = exchange(jnp.broadcast_to(right_moved, (nr,) + right_moved.shape), "res")
    q, rows, right_out = first(left_all, w, pairwise_cotangent, inv_count)
    right_in = exchange(right_out, "res")
    h, rt, left_out = second(right_all, w, pairwise_cotangent, inv_count)
    left_in = exchange(left_out, "seq")
    wo = third(rows, h, width)
    pairwise_update = fourth(rt, q, bias)
    right_total = lax.ppermute(total(right_in), ("seq", "res"), back)
    alignment_gradient, payload = after(left_in, right_total, homolog_matrix, factor_matrix, wo)
    summed = total_copies(exchange(payload, "res"), nq)
    summed = total_copies(exchange(summed, "seq"), nr)
    factor_matrix_deriv, output_weight_gradient = last(exchange(summed, "res"), factor_matrix.shape)
    return (pairwise_update, alignment_gradient, factor_matrix_deriv, output_weight_gradient)


def solution(mesh):
    placed = (P("seq", "res", None), P(), P(), P(), P("res", "seq", None))
    return jax.shard_map(
        functools.partial(body, mesh.shape["seq"], mesh.shape["res"]),
        mesh=mesh,
        in_specs=placed,
        out_specs=(P("res", "seq", None), P("seq", "res", None), P(), P()),
        check_vma=False,
    )
```

time: 792 us -> 173 us (0.22)
  waiting for transfers between devices: 479 us -> 16 us
  matrix products: 71.7 us -> 0 us
  blocking collectives: 113 us -> 45.5 us
  local copies, waits for them, and re-layouts: 74 us -> 6.54 us
  Pallas kernels: 0 us -> 51 us
  starting transfers between devices: 24.9 us -> 52.1 us
  between operations: 14.3 us -> 0.78 us
    psum x1 -> x0, waiting for transfers between devices: 270 us -> none  [body(): lax.psum((proj_partial, wo_partial), ('seq', 'res'))]
    reduce_scatter x1 -> x0, waiting for transfers between devices: 209 us -> none  [body(): lax.psum_scatter(left_partial, 'seq', scatter_dimension=0, tiled=True)]
    all_gather x2 -> x0, blocking collectives: 97.3 us -> none  [the longest x1 50 us: body(): spread = lax.all_gather(right_proj, 'res', axis=1, tiled=True)]
    dot_general x51 -> x0, matrix products: 71.7 us -> none  [the longest x8 17.4 us: tile_step(): jnp.einsum('ijcd,sic->sjd', grad_tile, left_block, preferred_element_type...]
    pallas_call x0 -> x10, Pallas kernels: none -> 51 us  [the longest x1 15 us: second(): pl.pallas_call(functools.partial(second_kernel, inv_count), grid=(steps,)...]
    convert_element_type x16 -> x0, local copies, waits for them, and re-layouts: 33.7 us -> none  [the longest x8 22.8 us: tile_step(): grad_outer = jnp.einsum('pe,fe->pf', cot_block, output_weight, preferred_...]
    all_to_all x1 -> x2, blocking collectives: 15.7 us -> 45.5 us  [exchange(): return lax.all_to_all(parts, axis, 0, 0, tiled=True)]
    all_to_all x2 -> x5, starting transfers between devices: 24.8 us -> 50.8 us  [exchange(): return lax.all_to_all(parts, axis, 0, 0, tiled=True)]
  transfers between devices with their start and end apart: 4 -> 7, of which waited for: 2 -> 3; matrix products, arithmetic and copies ran while one was open for 1% -> 1% of each run, Pallas kernels for 0% -> 27%
where the time goes in v1:
time: 173 us; the launch traced here: 172 us
  starting transfers between devices  52.1 us (30%)
  Pallas kernels  51 us (29%)
  blocking collectives  45.5 us (26%)
  waiting for transfers between devices  16 us (9%)
  local copies, waits for them, and re-layouts  6.54 us (4%)
    all_to_all x5, starting transfers between devices, exchange(): return lax.all_to_all(parts, axis, 0, 0, tiled=True)  50.8 us
    all_to_all x2, blocking collectives, exchange(): return lax.all_to_all(parts, axis, 0, 0, tiled=True)  45.5 us
    all_to_all x5, waiting for transfers between devices, exchange(): return lax.all_to_all(parts, axis, 0, 0, tiled=True)  16 us
    pallas_call x1, Pallas kernels, second(): pl.pallas_call(functools.partial(second_kernel, inv_count), grid=(steps,)...  15 us
    pallas_call x1, Pallas kernels, first(): pl.pallas_call(functools.partial(first_kernel, inv_count), grid=(steps,),...  13.5 us
    pallas_call x1, Pallas kernels, fourth(): pl.pallas_call(fourth_kernel, grid=(steps,), in_specs=[whole(rt.shape), p...  10.5 us
    pallas_call x1, Pallas kernels, third(): pl.pallas_call(third_kernel, grid=(wide // block,), in_specs=[whole(rows....  7.73 us
    unnamed x16, local copies, waits for them, and re-layouts  4.73 us
  transfers between devices with their start and end apart: 7, of which 3 were waited for; matrix products, arithmetic and copies ran while one was open for 1% of the time, Pallas kernels for 27%

profile of v1, /device:TPU:1, one launch (start us, length us, event | category | flops | bytes accessed | tf_op | source)
XLA Modules:
  0.0 172.0 jit_solution(15774805708942528405)
XLA Ops:
  0.6 0.9 copy.9.factor_ref
  1.5 0.0 copy-start
  1.5 0.8 copy-done
  2.4 1.0 before.1
  3.4 16.2 %all-to-all-start.1 = ((bf16[16,32,128]{2,1,0:T(8,128)(2,1)}), bf16[16,32,128]{2,1,0:T(8,128)(2,1)S(1)}, u32[]{:S(2)}, u32[]{:S(2)}) async-start(bf16[16,32,128]{2,1,0:T(8,128)(2,1)} %get-tuple-element.18), calls=%async_computation.1 | async-start | bytes 262144 | tf_op jit(solution)/shard_map/all_to_all | solution.py:408
  19.6 0.7 collective-permute-start
  20.3 1.1 reshape.14.w_ref
  21.4 0.0 collective-permute-done
  21.4 9.7 %all-to-all-done.1.recv_ref = bf16[16,32,128]{2,1,0:T(8,128)(2,1)S(1)} async-done(((bf16[16,32,128]{2,1,0:T(8,128)(2,1)}), bf16[16,32,128]{2,1,0:T(8,128)(2,1)S(1)}, u32[]{:S(2)}, u32[]{:S(2)}) %all-to-all-start.1) | async-done | bytes 131104 | tf_op jit(solution)/shard_map/all_to_all | solution.py:408
  31.0 0.7 broadcast_in_dim.3
  31.8 10.1 %all-to-all-start = ((bf16[32,32,128]{2,1,0:T(8,128)(2,1)}), bf16[32,32,128]{2,1,0:T(8,128)(2,1)S(1)}, u32[]{:S(2)}, u32[]{:S(2)}) async-start(bf16[32,32,128]{2,1,0:T(8,128)(2,1)} %broadcast_in_dim.3), calls=%async_computation | async-start | bytes 524288 | tf_op jit(solution)/shard_map/all_to_all | solution.py:408
  41.9 0.0 copy-start.2
  41.9 1.6 copy-done.2
  43.5 0.0 copy-start.3
  43.5 13.5 %first.1 = (bf16[8,1024,1024]{2,1,0:T(8,128)(2,1)}, bf16[2048,128]{1,0:T(8,128)(2,1)S(1)}, bf16[32,32,128]{2,1,0:T(8,128)(2,1)}) custom-call(bf16[16,32,128]{2,1,0:T(8,128)(2,1)S(1)} %all-to-all-done.1.recv_ref, bf16[32,4096]{1,0:T(8,128)(2,1)S(1)} %reshape.14.w_ref, bf16[64,128,128]{2,1,0:T(8,128)(2,1)S(1)} %copy-done.2), custom_call_target="tpu_custom_call" | custom-call | flops 40000000000 | bytes 20000000 | tf_op jit(solution)/shard_map/first/pallas_call | solution.py:105
  57.0 0.0 all-to-all-done.recv_ref
  57.0 7.7 %all-to-all-start.3 = ((bf16[32,32,128]{2,1,0:T(8,128)(2,1)}), bf16[32,32,128]{2,1,0:T(8,128)(2,1)S(1)}, u32[]{:S(2)}, u32[]{:S(2)}) async-start(bf16[32,32,128]{2,1,0:T(8,128)(2,1)} %get-tuple-element.21), calls=%async_computation.3 | async-start | bytes 524288 | tf_op jit(solution)/shard_map/all_to_all | solution.py:408
  64.7 0.0 copy-done.3
  64.7 15.0 %second.1 = (bf16[2048,4096]{1,0:T(8,128)(2,1)}, bf16[1024,128]{1,0:T(8,128)(2,1)S(1)}, bf16[16,32,128]{2,1,0:T(8,128)(2,1)}) custom-call(bf16[32,32,128]{2,1,0:T(8,128)(2,1)S(1)} %all-to-all-done.recv_ref, bf16[32,4096]{1,0:T(8,128)(2,1)S(1)} %reshape.14.w_ref, bf16[64,128,128]{2,1,0:T(8,128)(2,1)S(1)} %copy-done.3), custom_call_target="tpu_custom_call" | custom-call | flops 40000000000 | bytes 20000000 | tf_op jit(solution)/shard_map/second/pallas_call | solution.py:191
  79.6 0.0 copy-start.5
  79.6 0.7 copy-done.5
  80.3 0.0 all-to-all-done.3.in_ref
  80.4 11.2 %all-to-all-start.2 = ((bf16[16,32,128]{2,1,0:T(8,128)(2,1)}), bf16[16,32,128]{2,1,0:T(8,128)(2,1)S(1)}, u32[]{:S(2)}, u32[]{:S(2)}) async-start(bf16[16,32,128]{2,1,0:T(8,128)(2,1)} %get-tuple-element.20), calls=%async_computation.2 | async-start | bytes 262144 | tf_op jit(solution)/shard_map/all_to_all | solution.py:408
  91.5 0.1 total.1
  91.6 0.7 collective-permute-start.1
  92.3 0.0 copy-start.1
  92.3 0.0 copy-start.4
  92.3 0.0 copy-start.6
  92.3 7.7 %third.1.wo_ref = bf16[32,32,128]{2,1,0:T(8,128)(2,1)S(1)} custom-call(bf16[2048,128]{1,0:T(8,128)(2,1)S(1)} %get-tuple-element.22.rows_ref, bf16[2048,4096]{1,0:T(8,128)(2,1)} %get-tuple-element.23.h_ref), custom_call_target="tpu_custom_call" | custom-call | flops 20000000000 | bytes 17000000 | tf_op jit(solution)/shard_map/third/pallas_call | solution.py:234
  100.0 2.8 %all-to-all-done.2.left_ref = bf16[16,32,128]{2,1,0:T(8,128)(2,1)S(1)} async-done(((bf16[16,32,128]{2,1,0:T(8,128)(2,1)}), bf16[16,32,128]{2,1,0:T(8,128)(2,1)S(1)}, u32[]{:S(2)}, u32[]{:S(2)}) %all-to-all-start.2) | async-done | bytes 131104 | tf_op jit(solution)/shard_map/all_to_all | solution.py:408
  102.9 0.0 collective-permute-done.1.right_ref
  102.9 0.0 copy-done.1
  102.9 1.1 after.1
  104.0 27.5 %all_to_all.35.in_ref = bf16[32,48,128]{2,1,0:T(8,128)(2,1)S(1)} all-to-all(bf16[32,48,128]{2,1,0:T(8,128)(2,1)S(1)} %get-tuple-element.25), channel_id=1, replica_groups=mesh['seq'=16,'res'=32] {'res'}, dimensions={0} | all-to-all | bytes 786432 | tf_op jit(solution)/shard_map/all_to_all | solution.py:408
  131.5 0.1 total_copies.2
  131.6 18.0 %all_to_all.36.in_ref = bf16[16,48,128]{2,1,0:T(8,128)(2,1)S(1)} all-to-all(bf16[16,48,128]{2,1,0:T(8,128)(2,1)S(1)} %total_copies.2), channel_id=1, replica_groups=mesh['seq'=16,'res'=32] {'seq'}, dimensions={0} | all-to-all | bytes 393216 | tf_op jit(solution)/shard_map/all_to_all | solution.py:408
  149.5 0.8 total_copies.3
  150.3 5.6 %all-to-all-start.6 = ((bf16[32,48,128]{2,1,0:T(8,128)(2,1)}), bf16[32,48,128]{2,1,0:T(8,128)(2,1)S(1)}, u32[]{:S(2)}, u32[]{:S(2)}) async-start(bf16[32,48,128]{2,1,0:T(8,128)(2,1)} %total_copies.3), calls=%async_computation.6 | async-start | bytes 786432 | tf_op jit(solution)/shard_map/all_to_all | solution.py:408
  156.0 0.0 copy-done.4
  156.0 0.0 copy-done.6
  156.0 10.5 %fourth.1 = bf16[64,128,128]{2,1,0:T(8,128)(2,1)} custom-call(bf16[1024,128]{1,0:T(8,128)(2,1)S(1)} %copy-done.6, bf16[8,1024,1024]{2,1,0:T(8,128)(2,1)} %get-tuple-element.19.q_ref, f32[1,128]{1,0:T(1,128)S(1)} %bitcast.1), custom_call_target="tpu_custom_call" | custom-call | flops 20000000000 | bytes 19000000 | tf_op jit(solution)/shard_map/fourth/pallas_call | solution.py:266
  166.5 3.5 %all-to-all-done.6.in_ref = bf16[32,48,128]{2,1,0:T(8,128)(2,1)S(1)} async-done(((bf16[32,48,128]{2,1,0:T(8,128)(2,1)}), bf16[32,48,128]{2,1,0:T(8,128)(2,1)S(1)}, u32[]{:S(2)}, u32[]{:S(2)}) %all-to-all-start.6) | async-done | bytes 393248 | tf_op jit(solution)/shard_map/all_to_all | solution.py:408
  170.0 1.3 last.1
  171.3 0.7 copy.11
Async XLA Ops:
  1.5 0.8 copy-start
  3.4 27.7 %all-to-all-start.1 = ((bf16[16,32,128]{2,1,0:T(8,128)(2,1)}), bf16[16,32,128]{2,1,0:T(8,128)(2,1)S(1)}, u32[]{:S(2)}, u32[]{:S(2)}) async-start(bf16[16,32,128]{2,1,0:T(8,128)(2,1)} %get-tuple-element.18), calls=%async_computation.1 | async-start | bytes 262144 | tf_op jit(solution)/shard_map/all_to_all | solution.py:408
  19.6 1.7 %collective-permute-start = (bf16[32,128]{1,0:T(8,128)(2,1)S(1)}, bf16[32,128]{1,0:T(8,128)(2,1)S(1)}, u32[]{:S(2)}, u32[]{:S(2)}) collective-permute-start(bf16[32,128]{1,0:T(8,128)(2,1)S(1)} %get-tuple-element.16), channel_id=1, source_target_pairs={{0,0},{1,1},{2,32},{3,33},{4,64},{5,65},{6,96},{7,97},{8,128},{9,1... | collective-permute-start | bytes 24584 | tf_op jit(solution)/shard_map/ppermute | solution.py:419
  31.8 25.2 %all-to-all-start = ((bf16[32,32,128]{2,1,0:T(8,128)(2,1)}), bf16[32,32,128]{2,1,0:T(8,128)(2,1)S(1)}, u32[]{:S(2)}, u32[]{:S(2)}) async-start(bf16[32,32,128]{2,1,0:T(8,128)(2,1)} %broadcast_in_dim.3), calls=%async_computation | async-start | bytes 524288 | tf_op jit(solution)/shard_map/all_to_all | solution.py:408
  41.9 1.6 copy-start.2
  43.5 21.2 %copy-start.3 = (bf16[64,128,128]{2,1,0:T(8,128)(2,1)S(1)}, bf16[64,128,128]{2,1,0:T(8,128)(2,1)}, u32[]{:S(2)}) copy-start(bf16[64,128,128]{2,1,0:T(8,128)(2,1)} %cot_ref.3) | copy-start | bytes 6291460
  57.0 23.4 %all-to-all-start.3 = ((bf16[32,32,128]{2,1,0:T(8,128)(2,1)}), bf16[32,32,128]{2,1,0:T(8,128)(2,1)S(1)}, u32[]{:S(2)}, u32[]{:S(2)}) async-start(bf16[32,32,128]{2,1,0:T(8,128)(2,1)} %get-tuple-element.21), calls=%async_computation.3 | async-start | bytes 524288 | tf_op jit(solution)/shard_map/all_to_all | solution.py:408
  79.6 0.7 copy-start.5
  80.4 22.5 %all-to-all-start.2 = ((bf16[16,32,128]{2,1,0:T(8,128)(2,1)}), bf16[16,32,128]{2,1,0:T(8,128)(2,1)S(1)}, u32[]{:S(2)}, u32[]{:S(2)}) async-start(bf16[16,32,128]{2,1,0:T(8,128)(2,1)} %get-tuple-element.20), calls=%async_computation.2 | async-start | bytes 262144 | tf_op jit(solution)/shard_map/all_to_all | solution.py:408
  91.6 11.3 %collective-permute-start.1 = (f32[32,128]{1,0:T(8,128)S(1)}, f32[32,128]{1,0:T(8,128)S(1)}, u32[]{:S(2)}, u32[]{:S(2)}) collective-permute-start(f32[32,128]{1,0:T(8,128)S(1)} %total.1), channel_id=1, source_target_pairs={{0,0},{1,1},{32,2},{33,3},{64,4},{65,5},{96,6},{97,7},{128,8},{129... | collective-permute-start | bytes 49160 | tf_op jit(solution)/shard_map/ppermute | solution.py:428
  92.3 10.6 %copy-start.1 = (bf16[2,64,256]{2,1,0:T(8,128)(2,1)S(1)}, bf16[2,64,256]{2,1,0:T(8,128)(2,1)}, u32[]{:S(2)}) copy-start(bf16[2,64,256]{2,1,0:T(8,128)(2,1)} %x_ref.3) | copy-start | bytes 196612
  92.3 63.7 %copy-start.4 = (f32[128]{0:T(128)S(1)}, f32[128]{0:T(128)}, u32[]{:S(2)}) copy-start(f32[128]{0:T(128)} %param.8) | copy-start | bytes 1540
  92.3 63.7 %copy-start.6 = (bf16[1024,128]{1,0:T(8,128)(2,1)S(1)}, bf16[1024,128]{1,0:T(8,128)(2,1)}, u32[]{:S(2)}) copy-start(bf16[1024,128]{1,0:T(8,128)(2,1)} %copy-done.5) | copy-start | bytes 786436
  150.3 19.7 %all-to-all-start.6 = ((bf16[32,48,128]{2,1,0:T(8,128)(2,1)}), bf16[32,48,128]{2,1,0:T(8,128)(2,1)S(1)}, u32[]{:S(2)}, u32[]{:S(2)}) async-start(bf16[32,48,128]{2,1,0:T(8,128)(2,1)} %total_copies.3), calls=%async_computation.6 | async-start | bytes 786432 | tf_op jit(solution)/shard_map/all_to_all | solution.py:408

commit v2 on v0

v2 whole, which is shorter than its diff:
```python
import functools

import jax
import jax.numpy as jnp
from jax import lax
from jax.experimental import pallas as pl
from jax.experimental.pallas import tpu as pltpu
from jax.sharding import PartitionSpec as P

BF = jnp.bfloat16
F32 = jnp.float32
LANES = 128
MIB = 1024 * 1024
BIG = 56
NN = (((1,), (0,)), ((), ()))
NT = (((1,), (1,)), ((), ()))


def dot(a, b, dims=NN):
    return lax.dot_general(a, b, dims, preferred_element_type=F32)


def params(size=16):
    return pltpu.CompilerParams(vmem_limit_bytes=size * MIB)


def whole(shape):
    return pl.BlockSpec(shape, lambda *_: (0,) * len(shape))


def low_lanes(shape, width):
    return lax.broadcasted_iota(jnp.int32, shape, len(shape) - 1) < width


def cost(flops):
    return pl.CostEstimate(flops=flops, bytes_accessed=4_000_000, transcendentals=0)


def standardize(x_ref):
    seqs, residues, ch = x_ref.shape
    x = x_ref[...].reshape(seqs * residues, ch).astype(F32)
    centered = x - jnp.mean(x, axis=-1, keepdims=True)
    variance = jnp.mean(centered * centered, axis=-1, keepdims=True)
    scale = lax.rsqrt(variance + 1e-05)
    return centered * scale, scale


def before_kernel(x_ref, factor_ref, left_ref, packed_ref, held):
    normed = standardize(x_ref)[0].astype(BF)
    packed_ref[: normed.shape[0], :] = normed
    mapped = dot(normed, factor_ref[...], NT)
    rows, both = mapped.shape
    width = both // 2
    per = LANES // width
    padded = jnp.concatenate([mapped, jnp.zeros((rows, LANES - both), F32)], axis=1)
    turned = padded.T[width:both].astype(BF)
    parts = normed.shape[1] // LANES
    few = width // parts
    packed_ref[normed.shape[0] :, :] = jnp.concatenate([turned[k * few : (k + 1) * few] for k in range(parts)], axis=1)
    held[...] = padded
    lane = lax.broadcasted_iota(jnp.int32, (rows // per, LANES), 1)
    total = held[pl.ds(0, rows // per, stride=per), :]
    for low in range(1, per):
        part = pltpu.roll(held[pl.ds(low, rows // per, stride=per), :], low * width, 1)
        total = jnp.where(lane < low * width, total, part)
    left_ref[...] = total.astype(BF)


def before(x, factor):
    width = factor.shape[0] // 2
    rows = x.shape[0] * x.shape[1]
    return pl.pallas_call(
        before_kernel,
        out_shape=[
            jax.ShapeDtypeStruct((rows * width // LANES, LANES), BF),
            jax.ShapeDtypeStruct((rows + width * rows // x.shape[2], x.shape[2]), BF),
        ],
        scratch_shapes=[pltpu.VMEM((rows, LANES), F32)],
        compiler_params=params(BIG),
        name="before",
    )(x, factor)


def rows_of(ref, index, count):
    return ref.at[pl.ds(pl.multiple_of(index * count, count), count), :]


def grad_outer_kernel(parts, given_ref, cot_ref, out_ref, w_ref, wide, held, sems):
    residues, cols, ch = cot_ref.shape
    block = residues // parts
    count = out_ref.shape[0] // parts
    width = count // block
    group = LANES // width
    wide[...] = given_ref[...].astype(F32)
    depth = wide.shape[0] // width
    for d in range(depth):
        w_ref[d * width : (d + 1) * width, :] = wide[pl.ds(d, width, stride=depth), :].astype(BF)

    def copy(index):
        return pltpu.make_async_copy(rows_of(held, index, count), rows_of(out_ref, index, count), sems.at[index])

    def one(index, carry):
        for n in range(block // 2):
            cot = cot_ref[pl.ds(index * block + 2 * n, 2)].reshape(2 * cols, ch)
            for m in range(w_ref.shape[0] // LANES):
                piece = dot(w_ref[m * LANES : (m + 1) * LANES, :], cot, NT).astype(BF)
                for k in range(2):
                    row = pl.multiple_of(index * count + (2 * n + k) * width, width)
                    for g in range(group):
                        d = m * group + g
                        held[pl.ds(row, width), d * cols : (d + 1) * cols] = piece[
                            g * width : (g + 1) * width, k * cols : (k + 1) * cols
                        ]
        copy(index).start()
        return carry

    lax.fori_loop(0, parts, one, 0)
    lax.fori_loop(0, parts, lambda index, carry: copy(index).wait(), None)


def grad_outer(w, cot, width, parts=8):
    residues, cols, ch = cot.shape
    shape = (residues * width, w.shape[0] // width * cols)
    return pl.pallas_call(
        functools.partial(grad_outer_kernel, parts),
        in_specs=[whole(w.shape), whole(cot.shape)],
        out_specs=[pl.BlockSpec(memory_space=pl.ANY), whole(w.shape)],
        grid=(1,),
        out_shape=[jax.ShapeDtypeStruct(shape, BF), jax.ShapeDtypeStruct(w.shape, BF)],
        scratch_shapes=[pltpu.VMEM(w.shape, F32), pltpu.VMEM(shape, BF), pltpu.SemaphoreType.DMA((parts,))],
        compiler_params=params(BIG),
        cost_estimate=cost(8_000_000_000),
        name="grad_outer",
    )(w, cot)


def right_kernel(inv_count, parts, recv_ref, grad_ref, out_ref, held, sems, spread, rows, sums, totals):
    nq, tall, lanes = recv_ref.shape
    width = out_ref.shape[1]
    count = grad_ref.shape[0] // parts
    half = lanes // 2

    def copy(index):
        return pltpu.make_async_copy(rows_of(grad_ref, index, count), rows_of(held, index, count), sems.at[index])

    lax.fori_loop(0, parts, lambda index, carry: copy(index).start(), None)
    spread[...] = recv_ref[...].reshape(nq * tall, lanes).astype(F32) * inv_count
    for s in range(2):
        for t in range(tall // 2):
            rows[t * lanes // count, s * nq : (s + 1) * nq, t * lanes % count : t * lanes % count + lanes] = spread[
                pl.ds(s * (tall // 2) + t, nq, stride=tall), :
            ].astype(BF)
    sums[...] = jnp.zeros_like(sums)

    def one(index, carry):
        copy(index).wait()
        sums[...] += dot(rows[index], rows_of(held, index, count)[...])
        return carry

    lax.fori_loop(0, parts, one, 0)
    low = low_lanes((nq, lanes), half)
    for d in range(width):
        a = sums[:nq, d * lanes : (d + 1) * lanes]
        b = sums[nq:, d * lanes : (d + 1) * lanes]
        totals[pl.ds(d, nq, stride=2 * width), :] = jnp.where(low, a, pltpu.roll(b, half, 1))
        totals[pl.ds(width + d, nq, stride=2 * width), :] = jnp.where(low, pltpu.roll(a, half, 1), b)
    out_ref[...] = totals[...].reshape(out_ref.shape).astype(BF)


def right(recv, grad, width, inv_count, parts=8):
    nq, tall, lanes = recv.shape
    depth, wide = grad.shape
    out = (2 * nq, width, lanes)
    return pl.pallas_call(
        functools.partial(right_kernel, inv_count, parts),
        in_specs=[whole(recv.shape), pl.BlockSpec(memory_space=pl.ANY)],
        out_specs=whole(out),
        grid=(1,),
        out_shape=jax.ShapeDtypeStruct(out, BF),
        scratch_shapes=[
            pltpu.VMEM(grad.shape, BF),
            pltpu.SemaphoreType.DMA((parts,)),
            pltpu.VMEM((nq * tall, lanes), F32),
            pltpu.VMEM((parts, 2 * nq, depth // parts), BF),
            pltpu.VMEM((2 * nq, wide), F32),
            pltpu.VMEM((2 * nq * width, lanes), F32),
        ],
        compiler_params=params(BIG),
        cost_estimate=cost(8_000_000_000),
        name="right",
    )(recv, grad)


def left_kernel(inv_count, parts, recv_ref, grad_ref, rt_ref, out_ref, held, sems, spread, rows, totals):
    nr, width, lanes = recv_ref.shape
    nq = nr // 2
    tall = out_ref.shape[1]
    count = grad_ref.shape[0] // parts

    def copy(index):
        return pltpu.make_async_copy(rows_of(grad_ref, index, count), rows_of(held, index, count), sems.at[index])

    lax.fori_loop(0, parts, lambda index, carry: copy(index).start(), None)
    spread[...] = recv_ref[...].reshape(nr * width, lanes).astype(F32)
    low = low_lanes((nq, lanes), lanes // 2)
    for d in range(width):
        a = spread[pl.ds(d, nq, stride=2 * width), :]
        b = spread[pl.ds(width + d, nq, stride=2 * width), :]
        first = jnp.where(low, a, pltpu.roll(b, lanes // 2, 1)).astype(BF)
        second = jnp.where(low, pltpu.roll(a, lanes // 2, 1), b).astype(BF)
        rt_ref[(2 * d) * nq : (2 * d + 1) * nq, :] = first
        rt_ref[(2 * d + 1) * nq : (2 * d + 2) * nq, :] = second
        rows[:nq, d * lanes : (d + 1) * lanes] = first
        rows[nq:, d * lanes : (d + 1) * lanes] = second

    def one(index, carry):
        copy(index).wait()
        part = dot(rows[...], rows_of(held, index, count)[...], NT) * inv_count
        for k in range(count // lanes):
            for s in range(2):
                t = s * (tall // 2) + index * (count // lanes) + k
                totals[pl.ds(t, nq, stride=tall), :] = part[s * nq : (s + 1) * nq, k * lanes : (k + 1) * lanes]
        return carry

    lax.fori_loop(0, parts, one, 0)
    out_ref[...] = totals[...].reshape(out_ref.shape).astype(BF)


def left(recv, grad, inv_count, parts=8):
    nr, width, lanes = recv.shape
    nq = nr // 2
    deep, wide = grad.shape
    out = (nq, 2 * deep // lanes, lanes)
    return pl.pallas_call(
        functools.partial(left_kernel, inv_count, parts),
        in_specs=[whole(recv.shape), pl.BlockSpec(memory_space=pl.ANY)],
        out_specs=[whole((nr * width, lanes)), whole(out)],
        grid=(1,),
        out_shape=[jax.ShapeDtypeStruct((nr * width, lanes), BF), jax.ShapeDtypeStruct(out, BF)],
        scratch_shapes=[
            pltpu.VMEM(grad.shape, BF),
            pltpu.SemaphoreType.DMA((parts,)),
            pltpu.VMEM((nr * width, lanes), F32),
            pltpu.VMEM((nr, wide), BF),
            pltpu.VMEM((out[0] * out[1], lanes), F32),
        ],
        compiler_params=params(BIG),
        cost_estimate=cost(8_000_000_000),
        name="left",
    )(recv, grad)


def weight_kernel(inv_count, recv_ref, rt_ref, cot_ref, out_ref, rows_ref, spread, held, totals):
    step = pl.program_id(0)
    nq, tall, lanes = recv_ref.shape
    block, cols, ch = cot_ref.shape
    depth, width, _ = out_ref.shape
    seqs = 2 * nq
    group = lanes // seqs

    @pl.when(step == 0)
    def _():
        per = lanes // width
        spread[...] = recv_ref[...].reshape(nq * tall, lanes).astype(F32) * inv_count
        for t in range(tall // 2):
            for s in range(2):
                part = spread[pl.ds(s * (tall // 2) + t, nq, stride=tall), :]
                for low in range(per):
                    mine = part if low == 0 else pltpu.roll(part, lanes - low * width, 1)
                    row = ((t * per + low) * 2 + s) * nq
                    rows_ref[row : row + nq, :] = mine.astype(BF)

    cot = jnp.concatenate([cot_ref[i] for i in range(block)], axis=1)
    for m in range(depth // group):
        mine = rt_ref[m * lanes : (m + 1) * lanes, :]
        for n in range(block // 2):
            piece = dot(mine, cot[:, n * 2 * ch : (n + 1) * 2 * ch]).astype(BF)
            for g in range(group):
                d = m * group + g
                for k in range(2):
                    i = 2 * n + k
                    held[i * seqs : (i + 1) * seqs, d * ch : (d + 1) * ch] = piece[
                        g * seqs : (g + 1) * seqs, k * ch : (k + 1) * ch
                    ]
    count = block * seqs
    start = pl.multiple_of(step * count, count)
    turned = jnp.concatenate(
        [
            rows_ref[pl.ds(start + k * lanes, lanes), :].astype(F32).T[:width].astype(BF)
            for k in range(count // lanes)
        ],
        axis=1,
    )
    part = dot(turned, held[...])

    @pl.when(step == 0)
    def _():
        totals[...] = part

    @pl.when(step > 0)
    def _():
        totals[...] += part

    @pl.when(step == pl.num_programs(0) - 1)
    def _():
        for d in range(depth):
            out_ref[d] = totals[:, d * ch : (d + 1) * ch].astype(BF)


def weight(recv, rt, cot, width, inv_count, block=8):
    nq, tall, lanes = recv.shape
    residues, cols, ch = cot.shape
    seqs = 2 * nq
    depth = rt.shape[0] // seqs
    out = (depth, width, ch)
    return pl.pallas_call(
        functools.partial(weight_kernel, inv_count),
        grid=(residues // block,),
        in_specs=[whole(recv.shape), whole(rt.shape), pl.BlockSpec((block, cols, ch), lambda s: (s, 0, 0))],
        out_specs=[whole(out), whole((residues * seqs, lanes))],
        out_shape=[jax.ShapeDtypeStruct(out, BF), jax.ShapeDtypeStruct((residues * seqs, lanes), BF)],
        scratch_shapes=[
            pltpu.VMEM((nq * tall, lanes), F32),
            pltpu.VMEM((block * seqs, depth * ch), BF),
            pltpu.VMEM((width, depth * ch), F32),
        ],
        compiler_params=params(BIG),
        cost_estimate=cost(16_000_000_000),
        name="weight",
    )(recv, rt, cot)


def pair_kernel(rows_ref, w_ref, rt_ref, bias_ref, *refs):
    out_ref, token_ref, r, held = refs[-4:]
    block, cols, ch = out_ref.shape
    depth = held.shape[0]
    seqs = rows_ref.shape[0] // block
    width = w_ref.shape[0] * seqs // depth

    @pl.when(pl.program_id(0) == 0)
    def _():
        token_ref[...] = jnp.zeros_like(token_ref)
        for k in range(depth // LANES):
            r[:, k * LANES : (k + 1) * LANES] = rt_ref[k * LANES : (k + 1) * LANES, :].astype(F32).T.astype(BF)

    rows = rows_ref[:, :width]
    for n in range(depth // seqs // 2):
        w = jnp.concatenate([w_ref[(2 * n + k) * width : (2 * n + k + 1) * width, :] for k in range(2)], axis=1)
        piece = dot(rows, w).astype(BF)
        for k in range(2):
            d = 2 * n + k
            for i in range(block):
                held[d * seqs : (d + 1) * seqs, i * ch : (i + 1) * ch] = piece[
                    i * seqs : (i + 1) * seqs, k * ch : (k + 1) * ch
                ]
    bias = bias_ref[...]
    mine = r[...]
    for n in range(block // 2):
        piece = dot(mine, held[:, n * 2 * ch : (n + 1) * 2 * ch])
        for k in range(2):
            out_ref[2 * n + k] = (piece[:, k * ch : (k + 1) * ch] + bias).astype(BF)


def pair_part(rows, w, rt, bias, residues, begin, end, behind, held=None, block=8):
    count, lanes = rows.shape
    seqs = count // residues
    depth, cols = rt.shape
    ch = bias.shape[1]
    anywhere = pl.BlockSpec(memory_space=pl.ANY)
    more = [behind] + ([] if held is None else [held])
    return pl.pallas_call(
        pair_kernel,
        grid=(end - begin,),
        in_specs=[
            pl.BlockSpec((block * seqs, lanes), lambda s: (s + begin, 0)),
            whole(w.shape),
            whole(rt.shape),
            whole(bias.shape),
        ]
        + [anywhere] * len(more),
        out_specs=[pl.BlockSpec((block, cols, ch), lambda s: (s + begin, 0, 0)), whole((8, LANES))],
        out_shape=[
            jax.ShapeDtypeStruct((residues, cols, ch), BF),
            jax.ShapeDtypeStruct((8, LANES), F32),
        ],
        scratch_shapes=[pltpu.VMEM((cols, depth), BF), pltpu.VMEM((depth, block * ch), BF)],
        input_output_aliases={} if held is None else {5: 0},
        compiler_params=params(BIG),
        cost_estimate=cost(6_000_000_000),
        name="pair_part",
    )(rows, w, rt, bias, *more)


def left_rows(left_ref, held):
    added = jnp.sum(left_ref[...].astype(F32), axis=0)
    per = held.shape[0] // added.shape[0]
    width = LANES // per
    for low in range(per):
        part = added if low == 0 else pltpu.roll(added, LANES - low * width, 1)
        held[pl.ds(low, added.shape[0], stride=per), :] = part


def payload_kernel(left_ref, right_ref, normed_ref, moved_ref, wo_ref, out_ref, held):
    left_rows(left_ref, held)
    chunks, width, _ = wo_ref.shape
    left_grad = held[...].T[:width].astype(BF)
    factor_part = jnp.concatenate(
        [dot(left_grad, normed_ref[: held.shape[0], :]), dot(right_ref[...].astype(BF), moved_ref[: held.shape[0], :])], axis=0
    )
    stacked = jnp.concatenate(
        [factor_part[:, k * LANES : (k + 1) * LANES] for k in range(factor_part.shape[1] // LANES)], axis=0
    )
    coarse = stacked.astype(BF)
    fine = (stacked - coarse.astype(F32)).astype(BF)
    rows = stacked.shape[0] // chunks
    for k in range(chunks):
        mine = slice(k * rows, (k + 1) * rows)
        out_ref[k] = jnp.concatenate([wo_ref[k], coarse[mine], fine[mine]], axis=0)


def payload_of(left, right, normed, moved, wo):
    chunks, width, lanes = wo.shape
    rows, ch = left.shape[1] * lanes // width, normed.shape[1]
    extra = 2 * (2 * width * ch // lanes // chunks)
    return pl.pallas_call(
        payload_kernel,
        out_shape=jax.ShapeDtypeStruct((chunks, width + extra, lanes), BF),
        scratch_shapes=[pltpu.VMEM((rows, LANES), F32)],
        compiler_params=params(),
        name="payload",
    )(left, right, normed, moved, wo)


def align_kernel(left_ref, right_ref, x_ref, factor_ref, behind_ref, grad_ref, held):
    del behind_ref
    left_rows(left_ref, held)
    right_grad = right_ref[...]
    width, rows = right_grad.shape
    padded = jnp.concatenate([right_grad, jnp.zeros((LANES - width, rows), F32)], axis=0)
    lane = lax.broadcasted_iota(jnp.int32, (rows, LANES), 1)
    both = jnp.where(lane < width, held[...], pltpu.roll(padded.T, width, 1))
    normed, scale = standardize(x_ref)
    deriv = dot(both[:, : 2 * width].astype(BF), factor_ref[...])
    mean = jnp.mean(deriv, axis=-1, keepdims=True)
    along = jnp.mean(deriv * normed, axis=-1, keepdims=True)
    grad_ref[...] = (scale * (deriv - mean - normed * along)).astype(BF).reshape(grad_ref.shape)


def align(left, right, x, factor, behind):
    return pl.pallas_call(
        align_kernel,
        grid=(1,),
        in_specs=[whole(v.shape) for v in (left, right, x, factor, behind)],
        out_specs=whole(x.shape),
        out_shape=jax.ShapeDtypeStruct(x.shape, BF),
        scratch_shapes=[pltpu.VMEM((x.shape[0] * x.shape[1], LANES), F32)],
        compiler_params=params(),
        name="align",
    )(left, right, x, factor, behind)


def total_kernel(in_ref, out_ref):
    out_ref[...] = jnp.sum(in_ref[...].astype(F32), axis=0)


def total(parts):
    return pl.pallas_call(
        total_kernel,
        out_shape=jax.ShapeDtypeStruct(parts.shape[1:], F32),
        compiler_params=params(),
        name="total",
    )(parts)


def hold_kernel(in_ref, behind_ref, out_ref):
    del behind_ref
    out_ref[...] = in_ref[...]


def hold(value, behind):
    return pl.pallas_call(
        hold_kernel,
        grid=(1,),
        in_specs=[whole(value.shape), pl.BlockSpec(memory_space=pl.ANY)],
        out_specs=whole(value.shape),
        out_shape=jax.ShapeDtypeStruct(value.shape, value.dtype),
        compiler_params=params(),
        name="hold",
    )(value, behind)


def refine(parts, width):
    added = jnp.sum(parts, axis=0)
    mid = (added.shape[0] + width) // 2
    return added[:width], added[width:mid] + added[mid:]


def total_copies_kernel(width, in_ref, behind_ref, out_ref):
    del behind_ref
    main, rest = refine(in_ref[...].astype(F32), width)
    coarse = rest.astype(BF)
    fine = (rest - coarse.astype(F32)).astype(BF)
    summed = jnp.concatenate([main.astype(BF), coarse, fine], axis=0)
    for k in range(out_ref.shape[0]):
        out_ref[k] = summed


def total_copies(parts, width, copies, behind):
    return pl.pallas_call(
        functools.partial(total_copies_kernel, width),
        in_specs=[whole(parts.shape), whole(behind.shape)],
        out_specs=whole((copies,) + parts.shape[1:]),
        grid=(1,),
        out_shape=jax.ShapeDtypeStruct((copies,) + parts.shape[1:], BF),
        compiler_params=params(),
        name="total_copies",
    )(parts, behind)


def last_kernel(in_ref, factor_ref, weight_ref):
    chunks, tall, lanes = in_ref.shape
    width = weight_ref.shape[0] // chunks
    mid = (tall + width) // 2
    rest = []
    for d in range(chunks):
        weight_ref[pl.ds(d, width, stride=chunks), :] = in_ref[d, :width, :].astype(F32)
        tail = in_ref[d, width:, :].astype(F32)
        rest.append(tail[: mid - width] + tail[mid - width :])
    stacked = jnp.concatenate(rest, axis=0)
    both, ch = factor_ref.shape
    for k in range(ch // lanes):
        factor_ref[:, k * lanes : (k + 1) * lanes] = stacked[k * both : (k + 1) * both]


def last(parts, width, factor_shape):
    chunks, tall, lanes = parts.shape
    return pl.pallas_call(
        last_kernel,
        out_shape=[
            jax.ShapeDtypeStruct(factor_shape, F32),
            jax.ShapeDtypeStruct((chunks * width, lanes), F32),
        ],
        compiler_params=params(),
        name="last",
    )(parts)


def exchange(parts, axis):
    return lax.all_to_all(parts, axis, 0, 0, tiled=True)


def exchange_in(parts, groups):
    return lax.all_to_all(parts, ("seq", "res"), 0, 0, axis_index_groups=groups, tiled=True)


def grouped(pairs, nr, key):
    found = {}
    for a, b in pairs:
        found.setdefault(key(a, b), []).append(a * nr + b)
    return list(found.values())


def body(nq, nr, homolog_matrix, factor_matrix, output_weight, output_bias, pairwise_cotangent):
    width = factor_matrix.shape[1] // 2
    inv_count = 1.0 / (2 * nq)
    pairs = [(a, b) for a in range(nq) for b in range(nr)]
    line = nq // 2
    outer = grouped(pairs, nr, lambda a, b: (a % line, b % 2))
    inner = grouped(pairs, nr, lambda a, b: (a // line, b // 2))
    there = [(s * nr + r, (r // 2) * nr + 2 * s + r % 2) for s in range(nq) for r in range(nr)]
    back = [(b, a) for a, b in there]
    bias = output_bias.reshape(1, -1)
    factor = factor_matrix.T
    left_mine, packed = before(homolog_matrix, factor)
    moved = lax.ppermute(packed, ("seq", "res"), there)
    left_all = exchange(jnp.broadcast_to(left_mine, (nq,) + left_mine.shape), "seq")
    tail = moved[homolog_matrix.shape[0] * homolog_matrix.shape[1] :]
    right_moved = jnp.concatenate(jnp.split(tail, tail.shape[1] // LANES, axis=1), axis=0)
    grad, w = grad_outer(output_weight, pairwise_cotangent, width)
    right_all = exchange(jnp.broadcast_to(right_moved, (nr,) + right_moved.shape), "res")
    right_in = exchange(right(left_all, grad, width, inv_count), "res")
    rt, left_out = left(right_all, grad, inv_count)
    left_in = exchange(left_out, "seq")
    wo, rows = weight(left_all, rt, pairwise_cotangent, width, inv_count)
    right_total = total(right_in)
    payload = payload_of(left_in, right_total, packed, moved, wo)
    residues = pairwise_cotangent.shape[0]
    steps = residues // 8
    cuts = [0, (steps + 2) // 3, (2 * steps + 2) // 3, steps]
    summed = exchange_in(payload, outer)
    pair, token = pair_part(rows, w, rt, bias, residues, cuts[0], cuts[1], payload)
    payload = total_copies(summed, width, len(inner[0]), token)
    summed = exchange_in(payload, inner)
    pair, token = pair_part(rows, w, rt, bias, residues, cuts[1], cuts[2], payload, pair)
    payload = total_copies(summed, width, len(outer[0]), token)
    summed = exchange_in(payload, outer)
    right_back = lax.ppermute(hold(right_total, payload), ("seq", "res"), back)
    pairwise_update, token = pair_part(rows, w, rt, bias, residues, cuts[2], cuts[3], payload, pair)
    alignment_gradient = align(left_in, right_back, homolog_matrix, factor, token)
    factor_grad, output_weight_gradient = last(summed, width, factor.shape)
    return (pairwise_update, alignment_gradient, factor_grad.T, output_weight_gradient)


def solution(mesh):
    placed = (P("seq", "res", None), P(), P(), P(), P("res", "seq", None))
    return jax.shard_map(
        functools.partial(body, mesh.shape["seq"], mesh.shape["res"]),
        mesh=mesh,
        in_specs=placed,
        out_specs=(P("res", "seq", None), P("seq", "res", None), P(), P()),
        check_vma=False,
    )
```

time: 792 us -> 163 us (0.21)
  waiting for transfers between devices: 479 us -> 26.8 us
  blocking collectives: 113 us -> 0 us
  matrix products: 71.7 us -> 0 us
  local copies, waits for them, and re-layouts: 74 us -> 5.14 us
  Pallas kernels: 0 us -> 60.6 us
  starting transfers between devices: 24.9 us -> 66.7 us
  between operations: 14.3 us -> 0.84 us
    psum x1 -> x0, waiting for transfers between devices: 270 us -> none  [body(): lax.psum((proj_partial, wo_partial), ('seq', 'res'))]
    reduce_scatter x1 -> x0, waiting for transfers between devices: 209 us -> none  [body(): lax.psum_scatter(left_partial, 'seq', scatter_dimension=0, tiled=True)]
    all_gather x2 -> x0, blocking collectives: 97.3 us -> none  [the longest x1 50 us: body(): spread = lax.all_gather(right_proj, 'res', axis=1, tiled=True)]
    dot_general x51 -> x0, matrix products: 71.7 us -> none  [the longest x8 17.4 us: tile_step(): jnp.einsum('ijcd,sic->sjd', grad_tile, left_block, preferred_element_type...]
    pallas_call x0 -> x15, Pallas kernels: none -> 60.6 us  [the longest x3 14 us: pair_part(): pl.pallas_call(pair_kernel, grid=(end - begin,), in_specs=[pl.BlockSpec((...]
    all_to_all x2 -> x7, starting transfers between devices: 24.8 us -> 64.5 us  [the longest x4 43.2 us: exchange(): return lax.all_to_all(parts, axis, 0, 0, tiled=True)]
    convert_element_type x16 -> x0, local copies, waits for them, and re-layouts: 33.7 us -> none  [the longest x8 22.8 us: tile_step(): grad_outer = jnp.einsum('pe,fe->pf', cot_block, output_weight, preferred_...]
    all_to_all x2 -> x7, waiting for transfers between devices: 0.01 us -> 26.8 us  [the longest x3 20.8 us: exchange_in(): lax.all_to_all(parts, ('seq', 'res'), 0, 0, axis_index_groups=groups, til...]
  transfers between devices with their start and end apart: 4 -> 9, of which waited for: 2 -> 6; matrix products, arithmetic and copies ran while one was open for 1% -> 1% of each run, Pallas kernels for 0% -> 34%
where the time goes in v2:
time: 163 us; the launch traced here: 160 us
  starting transfers between devices  66.7 us (41%)
  Pallas kernels  60.6 us (37%)
  waiting for transfers between devices  26.8 us (16%)
  local copies, waits for them, and re-layouts  5.14 us (3%)
    all_to_all x4, starting transfers between devices, exchange(): return lax.all_to_all(parts, axis, 0, 0, tiled=True)  43.2 us
    all_to_all x3, starting transfers between devices, exchange_in(): lax.all_to_all(parts, ('seq', 'res'), 0, 0, axis_index_groups=groups, til...  21.3 us
    all_to_all x3, waiting for transfers between devices, exchange_in(): lax.all_to_all(parts, ('seq', 'res'), 0, 0, axis_index_groups=groups, til...  20.8 us
    pallas_call x3, Pallas kernels, pair_part(): pl.pallas_call(pair_kernel, grid=(end - begin,), in_specs=[pl.BlockSpec((...  14 us
    pallas_call x1, Pallas kernels, weight(): pl.pallas_call(functools.partial(weight_kernel, inv_count), grid=(residue...  12 us
    pallas_call x1, Pallas kernels, grad_outer(): pl.pallas_call(functools.partial(grad_outer_kernel, parts), in_specs=[who...  9.96 us
    pallas_call x1, Pallas kernels, left(): pl.pallas_call(functools.partial(left_kernel, inv_count, parts), in_specs...  9.32 us
    pallas_call x1, Pallas kernels, right(): pl.pallas_call(functools.partial(right_kernel, inv_count, parts), in_spec...  8.56 us
  transfers between devices with their start and end apart: 9, of which 6 were waited for; matrix products, arithmetic and copies ran while one was open for 1% of the time, Pallas kernels for 34%

profile of v2, /device:TPU:1, one launch (start us, length us, event | category | flops | bytes accessed | tf_op | source)
XLA Modules:
  0.0 160.0 jit_solution(16164993979955325926)
XLA Ops:
  0.6 1.9 %before.1 = (bf16[32,128]{1,0:T(8,128)(2,1)}, bf16[144,256]{1,0:T(8,128)(2,1)}) custom-call(bf16[2,64,256]{2,1,0:T(8,128)(2,1)} %x_ref.3, bf16[64,256]{1,0:T(8,128)(2,1)} %bitcast.3), custom_call_target="tpu_custom_call" | custom-call | tf_op jit(solution)/shard_map/before/pallas_call | solution.py:72
  2.5 1.5 collective-permute-start
  4.0 1.4 broadcast_in_dim.6
  5.4 16.6 %all-to-all-start = ((bf16[16,32,128]{2,1,0:T(8,128)(2,1)}), bf16[16,32,128]{2,1,0:T(8,128)(2,1)S(1)}, u32[]{:S(2)}, u32[]{:S(2)}) async-start(bf16[16,32,128]{2,1,0:T(8,128)(2,1)} %broadcast_in_dim.6), calls=%async_computation | async-start | bytes 262144 | tf_op jit(solution)/shard_map/all_to_all | solution.py:549
  22.0 10.0 %grad_outer.1 = (bf16[2048,4096]{1,0:T(8,128)(2,1)}, bf16[1024,128]{1,0:T(8,128)(2,1)}) custom-call(bf16[1024,128]{1,0:T(8,128)(2,1)} %given_ref.1, bf16[64,128,128]{2,1,0:T(8,128)(2,1)} %cot_ref.3), custom_call_target="tpu_custom_call" | custom-call | flops 8000000000 | bytes 4000000 | tf_op jit(solution)/shard_map/grad_outer/pallas_call | solution.py:124
  32.0 0.0 collective-permute-done.moved_ref
  32.0 1.3 all-to-all-done.recv_ref
  33.3 0.7 broadcast_in_dim.7
  34.1 12.2 %all-to-all-start.1 = ((bf16[32,32,128]{2,1,0:T(8,128)(2,1)}), bf16[32,32,128]{2,1,0:T(8,128)(2,1)S(1)}, u32[]{:S(2)}, u32[]{:S(2)}) async-start(bf16[32,32,128]{2,1,0:T(8,128)(2,1)} %broadcast_in_dim.7), calls=%async_computation.1 | async-start | bytes 524288 | tf_op jit(solution)/shard_map/all_to_all | solution.py:549
  46.3 0.0 copy-done.8
  46.3 8.6 %right.1 = bf16[32,32,128]{2,1,0:T(8,128)(2,1)} custom-call(bf16[16,32,128]{2,1,0:T(8,128)(2,1)} %copy-done.8, bf16[2048,4096]{1,0:T(8,128)(2,1)} %get-tuple-element.22.grad_ref), custom_call_target="tpu_custom_call" | custom-call | flops 8000000000 | bytes 4000000 | tf_op jit(solution)/shard_map/right/pallas_call | solution.py:174
  54.9 2.7 %all-to-all-done.1.recv_ref = bf16[32,32,128]{2,1,0:T(8,128)(2,1)S(1)} async-done(((bf16[32,32,128]{2,1,0:T(8,128)(2,1)}), bf16[32,32,128]{2,1,0:T(8,128)(2,1)S(1)}, u32[]{:S(2)}, u32[]{:S(2)}) %all-to-all-start.1) | async-done | bytes 262176 | tf_op jit(solution)/shard_map/all_to_all | solution.py:549
  57.6 5.0 %all-to-all-start.3 = ((bf16[32,32,128]{2,1,0:T(8,128)(2,1)}), bf16[32,32,128]{2,1,0:T(8,128)(2,1)S(1)}, u32[]{:S(2)}, u32[]{:S(2)}) async-start(bf16[32,32,128]{2,1,0:T(8,128)(2,1)} %right.1), calls=%async_computation.3 | async-start | bytes 524288 | tf_op jit(solution)/shard_map/all_to_all | solution.py:549
  62.6 0.0 copy-done.7
  62.6 9.3 %left.1 = (bf16[1024,128]{1,0:T(8,128)(2,1)}, bf16[16,32,128]{2,1,0:T(8,128)(2,1)}) custom-call(bf16[32,32,128]{2,1,0:T(8,128)(2,1)} %copy-done.7, bf16[2048,4096]{1,0:T(8,128)(2,1)} %get-tuple-element.22.grad_ref), custom_call_target="tpu_custom_call" | custom-call | flops 8000000000 | bytes 4000000 | tf_op jit(solution)/shard_map/left/pallas_call | solution.py:234
  72.0 1.9 %all-to-all-done.3.in_ref = bf16[32,32,128]{2,1,0:T(8,128)(2,1)S(1)} async-done(((bf16[32,32,128]{2,1,0:T(8,128)(2,1)}), bf16[32,32,128]{2,1,0:T(8,128)(2,1)S(1)}, u32[]{:S(2)}, u32[]{:S(2)}) %all-to-all-start.3) | async-done | bytes 262176 | tf_op jit(solution)/shard_map/all_to_all | solution.py:549
  73.9 9.3 %all-to-all-start.2 = ((bf16[16,32,128]{2,1,0:T(8,128)(2,1)}), bf16[16,32,128]{2,1,0:T(8,128)(2,1)S(1)}, u32[]{:S(2)}, u32[]{:S(2)}) async-start(bf16[16,32,128]{2,1,0:T(8,128)(2,1)} %get-tuple-element.26), calls=%async_computation.2 | async-start | bytes 262144 | tf_op jit(solution)/shard_map/all_to_all | solution.py:549
  83.2 0.0 copy-start.3
  83.2 12.0 %weight.1 = (bf16[32,32,128]{2,1,0:T(8,128)(2,1)}, bf16[2048,128]{1,0:T(8,128)(2,1)}) custom-call(bf16[16,32,128]{2,1,0:T(8,128)(2,1)} %copy-done.8, bf16[1024,128]{1,0:T(8,128)(2,1)} %get-tuple-element.23.rt_ref, bf16[64,128,128]{2,1,0:T(8,128)(2,1)} %cot_ref.3), custom_call_target="tpu_custom_call" | custom-call | flops 16000000000 | bytes 4000000 | tf_op jit(solution)/shard_map/weight/pallas_call | solution.py:316
  95.2 0.1 total.1.right_ref.in_ref
  95.3 0.0 all-to-all-done.2.left_ref
  95.3 0.0 copy-done.3
  95.3 0.0 copy-start
  95.3 0.9 copy-done
  96.2 1.0 payload.1.refs_0_
  97.3 7.7 %all-to-all-start.4 = ((bf16[32,40,128]{2,1,0:T(8,128)(2,1)}), bf16[32,40,128]{2,1,0:T(8,128)(2,1)S(1)}, u32[]{:S(2)}, u32[]{:S(2)}) async-start(bf16[32,40,128]{2,1,0:T(8,128)(2,1)} %payload.1.refs_0_), calls=%async_computation.4 | async-start | bytes 655360 | tf_op jit(solution)/shard_map/all_to_all | solution.py:553
  105.0 5.0 %pair_part.3 = (bf16[64,128,128]{2,1,0:T(8,128)(2,1)}, f32[8,128]{1,0:T(8,128)}) custom-call(bf16[2048,128]{1,0:T(8,128)(2,1)} %get-tuple-element.24.rows_ref, bf16[1024,128]{1,0:T(8,128)(2,1)} %get-tuple-element.25.w_ref, bf16[1024,128]{1,0:T(8,128)(2,1)} %get-tuple-element.23.rt_ref, f32[1,128]{1,0:T(1,128)} %bitcast.6, bf16[32,40,128]{2,1,0:T(8,128)(2,1)} %payload.1.refs_0_), custom_call_target="tpu_custom_call" | custom-call | flops 6000000000 | bytes 4000000 | tf_op jit(solution)/shard_map/pair_part/pallas_call | solution.py:371
  110.0 7.8 %all-to-all-done.4.in_ref = bf16[32,40,128]{2,1,0:T(8,128)(2,1)S(1)} async-done(((bf16[32,40,128]{2,1,0:T(8,128)(2,1)}), bf16[32,40,128]{2,1,0:T(8,128)(2,1)S(1)}, u32[]{:S(2)}, u32[]{:S(2)}) %all-to-all-start.4) | async-done | bytes 327712 | tf_op jit(solution)/shard_map/all_to_all | solution.py:553
  117.7 0.7 copy-done.6
  118.4 0.7 total_copies.2.refs_0_
  119.1 9.7 %all-to-all-start.5 = ((bf16[16,40,128]{2,1,0:T(8,128)(2,1)}), bf16[16,40,128]{2,1,0:T(8,128)(2,1)S(1)}, u32[]{:S(2)}, u32[]{:S(2)}) async-start(bf16[16,40,128]{2,1,0:T(8,128)(2,1)} %total_copies.2.refs_0_), calls=%async_computation.5 | async-start | bytes 327680 | tf_op jit(solution)/shard_map/all_to_all | solution.py:553
  128.9 5.0 %pair_part.4 = (bf16[64,128,128]{2,1,0:T(8,128)(2,1)}, f32[8,128]{1,0:T(8,128)}) custom-call(bf16[2048,128]{1,0:T(8,128)(2,1)} %get-tuple-element.24.rows_ref, bf16[1024,128]{1,0:T(8,128)(2,1)} %get-tuple-element.25.w_ref, bf16[1024,128]{1,0:T(8,128)(2,1)} %get-tuple-element.23.rt_ref, f32[1,128]{1,0:T(1,128)} %bitcast.7, ...), custom_call_target="tpu_custom_call", output_to_operand_aliasing={{0}: (5, {})} | custom-call | flops 6000000000 | bytes 4000000 | tf_op jit(solution)/shard_map/pair_part/pallas_call | solution.py:371
  133.9 4.6 %all-to-all-done.5.in_ref = bf16[16,40,128]{2,1,0:T(8,128)(2,1)S(1)} async-done(((bf16[16,40,128]{2,1,0:T(8,128)(2,1)}), bf16[16,40,128]{2,1,0:T(8,128)(2,1)S(1)}, u32[]{:S(2)}, u32[]{:S(2)}) %all-to-all-start.5) | async-done | bytes 163872 | tf_op jit(solution)/shard_map/all_to_all | solution.py:553
  138.5 0.7 copy-done.5
  139.2 0.8 total_copies.3.refs_0_.behind_ref
  140.0 3.9 %all-to-all-start.6 = ((bf16[32,40,128]{2,1,0:T(8,128)(2,1)}), bf16[32,40,128]{2,1,0:T(8,128)(2,1)S(1)}, u32[]{:S(2)}, u32[]{:S(2)}) async-start(bf16[32,40,128]{2,1,0:T(8,128)(2,1)} %total_copies.3.refs_0_.behind_ref), calls=%async_computation.6 | async-start | bytes 655360 | tf_op jit(solution)/shard_map/all_to_all | solution.py:553
  143.9 0.7 collective-permute-start.1
  144.6 0.0 copy-start.1
  144.6 0.0 copy-start.2
  144.6 4.0 %pair_part.5 = (bf16[64,128,128]{2,1,0:T(8,128)(2,1)}, f32[8,128]{1,0:T(8,128)}) custom-call(bf16[2048,128]{1,0:T(8,128)(2,1)} %get-tuple-element.24.rows_ref, bf16[1024,128]{1,0:T(8,128)(2,1)} %get-tuple-element.25.w_ref, bf16[1024,128]{1,0:T(8,128)(2,1)} %get-tuple-element.23.rt_ref, f32[1,128]{1,0:T(1,128)} %bitcast.8, ...), custom_call_target="tpu_custom_call", output_to_operand_aliasing={{0}: (5, {})} | custom-call | flops 6000000000 | bytes 4000000 | tf_op jit(solution)/shard_map/pair_part/pallas_call | solution.py:371
  148.6 0.0 collective-permute-done.1.right_ref
  148.6 0.0 copy-done.1
  148.6 0.0 copy-done.2
  148.6 0.0 copy-start.4
  148.6 0.7 copy-done.4
  149.3 1.0 align.1
  150.3 8.4 %all-to-all-done.6.in_ref = bf16[32,40,128]{2,1,0:T(8,128)(2,1)S(1)} async-done(((bf16[32,40,128]{2,1,0:T(8,128)(2,1)}), bf16[32,40,128]{2,1,0:T(8,128)(2,1)S(1)}, u32[]{:S(2)}, u32[]{:S(2)}) %all-to-all-start.6) | async-done | bytes 327712 | tf_op jit(solution)/shard_map/all_to_all | solution.py:553
  158.7 1.3 last.1
  (7 shorter events, 0.0 us)
Async XLA Ops:
  2.5 29.5 %collective-permute-start = (bf16[144,256]{1,0:T(8,128)(2,1)}, bf16[144,256]{1,0:T(8,128)(2,1)S(1)}, u32[]{:S(2)}, u32[]{:S(2)}) collective-permute-start(bf16[144,256]{1,0:T(8,128)(2,1)} %get-tuple-element.21.normed_ref), channel_id=1, source_target_pairs={{0,0},{1,1},{2,32},{3,33},{4,64},{5,65},{6,96},{7,97},{8,128},{9,1... | collective-permute-start | bytes 221192 | tf_op jit(solution)/shard_map/ppermute | solution.py:575
  5.4 27.9 %all-to-all-start = ((bf16[16,32,128]{2,1,0:T(8,128)(2,1)}), bf16[16,32,128]{2,1,0:T(8,128)(2,1)S(1)}, u32[]{:S(2)}, u32[]{:S(2)}) async-start(bf16[16,32,128]{2,1,0:T(8,128)(2,1)} %broadcast_in_dim.6), calls=%async_computation | async-start | bytes 262144 | tf_op jit(solution)/shard_map/all_to_all | solution.py:549
  33.3 13.0 %copy-start.8 = (bf16[16,32,128]{2,1,0:T(8,128)(2,1)}, bf16[16,32,128]{2,1,0:T(8,128)(2,1)S(1)}, u32[]{:S(2)}) copy-start(bf16[16,32,128]{2,1,0:T(8,128)(2,1)S(1)} %all-to-all-done.recv_ref) | copy-start | bytes 393220
  34.1 23.5 %all-to-all-start.1 = ((bf16[32,32,128]{2,1,0:T(8,128)(2,1)}), bf16[32,32,128]{2,1,0:T(8,128)(2,1)S(1)}, u32[]{:S(2)}, u32[]{:S(2)}) async-start(bf16[32,32,128]{2,1,0:T(8,128)(2,1)} %broadcast_in_dim.7), calls=%async_computation.1 | async-start | bytes 524288 | tf_op jit(solution)/shard_map/all_to_all | solution.py:549
  57.6 5.0 %copy-start.7 = (bf16[32,32,128]{2,1,0:T(8,128)(2,1)}, bf16[32,32,128]{2,1,0:T(8,128)(2,1)S(1)}, u32[]{:S(2)}) copy-start(bf16[32,32,128]{2,1,0:T(8,128)(2,1)S(1)} %all-to-all-done.1.recv_ref) | copy-start | bytes 786436
  57.6 16.3 %all-to-all-start.3 = ((bf16[32,32,128]{2,1,0:T(8,128)(2,1)}), bf16[32,32,128]{2,1,0:T(8,128)(2,1)S(1)}, u32[]{:S(2)}, u32[]{:S(2)}) async-start(bf16[32,32,128]{2,1,0:T(8,128)(2,1)} %right.1), calls=%async_computation.3 | async-start | bytes 524288 | tf_op jit(solution)/shard_map/all_to_all | solution.py:549
  73.9 21.3 %all-to-all-start.2 = ((bf16[16,32,128]{2,1,0:T(8,128)(2,1)}), bf16[16,32,128]{2,1,0:T(8,128)(2,1)S(1)}, u32[]{:S(2)}, u32[]{:S(2)}) async-start(bf16[16,32,128]{2,1,0:T(8,128)(2,1)} %get-tuple-element.26), calls=%async_computation.2 | async-start | bytes 262144 | tf_op jit(solution)/shard_map/all_to_all | solution.py:549
  83.2 12.1 %copy-start.3 = (bf16[144,256]{1,0:T(8,128)(2,1)S(1)}, bf16[144,256]{1,0:T(8,128)(2,1)}, u32[]{:S(2)}) copy-start(bf16[144,256]{1,0:T(8,128)(2,1)} %get-tuple-element.21.normed_ref) | copy-start | bytes 221188
  95.3 1.0 copy-start
  97.3 20.5 %all-to-all-start.4 = ((bf16[32,40,128]{2,1,0:T(8,128)(2,1)}), bf16[32,40,128]{2,1,0:T(8,128)(2,1)S(1)}, u32[]{:S(2)}, u32[]{:S(2)}) async-start(bf16[32,40,128]{2,1,0:T(8,128)(2,1)} %payload.1.refs_0_), calls=%async_computation.4 | async-start | bytes 655360 | tf_op jit(solution)/shard_map/all_to_all | solution.py:553
  117.7 0.7 copy-start.6
  119.1 19.4 %all-to-all-start.5 = ((bf16[16,40,128]{2,1,0:T(8,128)(2,1)}), bf16[16,40,128]{2,1,0:T(8,128)(2,1)S(1)}, u32[]{:S(2)}, u32[]{:S(2)}) async-start(bf16[16,40,128]{2,1,0:T(8,128)(2,1)} %total_copies.2.refs_0_), calls=%async_computation.5 | async-start | bytes 327680 | tf_op jit(solution)/shard_map/all_to_all | solution.py:553
  138.5 0.7 copy-start.5
  140.0 18.7 %all-to-all-start.6 = ((bf16[32,40,128]{2,1,0:T(8,128)(2,1)}), bf16[32,40,128]{2,1,0:T(8,128)(2,1)S(1)}, u32[]{:S(2)}, u32[]{:S(2)}) async-start(bf16[32,40,128]{2,1,0:T(8,128)(2,1)} %total_copies.3.refs_0_.behind_ref), calls=%async_computation.6 | async-start | bytes 655360 | tf_op jit(solution)/shard_map/all_to_all | solution.py:553
  143.9 4.7 %collective-permute-start.1 = (f32[32,128]{1,0:T(8,128)S(1)}, f32[32,128]{1,0:T(8,128)S(1)}, u32[]{:S(2)}, u32[]{:S(2)}) collective-permute-start(f32[32,128]{1,0:T(8,128)S(1)} %hold.1), channel_id=1, source_target_pairs={{0,0},{1,1},{32,2},{33,3},{64,4},{65,5},{96,6},{97,7},{128,8},{129... | collective-permute-start | bytes 49160 | tf_op jit(solution)/shard_map/ppermute | solution.py:597
  144.6 4.0 %copy-start.1 = (bf16[2,64,256]{2,1,0:T(8,128)(2,1)S(1)}, bf16[2,64,256]{2,1,0:T(8,128)(2,1)}, u32[]{:S(2)}) copy-start(bf16[2,64,256]{2,1,0:T(8,128)(2,1)} %x_ref.3) | copy-start | bytes 196612
  144.6 4.0 %copy-start.2 = (bf16[256,64]{0,1:T(8,128)(2,1)S(1)}, bf16[256,64]{0,1:T(8,128)(2,1)}, u32[]{:S(2)}) copy-start(bf16[256,64]{0,1:T(8,128)(2,1)} %param.6) | copy-start | bytes 98308
  148.6 0.7 copy-start.4

commit v3 on v2

--- a/solution.py
+++ b/solution.py
@@ -2,6 +2,7 @@
 
 import jax
 import jax.numpy as jnp
+import numpy as np
 from jax import lax
 from jax.experimental import pallas as pl
 from jax.experimental.pallas import tpu as pltpu
@@ -134,7 +135,7 @@
     )(w, cot)
 
 
-def right_kernel(inv_count, parts, recv_ref, grad_ref, out_ref, held, sems, spread, rows, sums, totals):
+def right_kernel(inv_count, parts, mine_ref, slots_ref, recv_ref, grad_ref, out_ref, held, sems, spread, rows, sums, totals):
     nq, tall, lanes = recv_ref.shape
     width = out_ref.shape[1]
     count = grad_ref.shape[0] // parts
@@ -164,16 +165,17 @@
         b = sums[nq:, d * lanes : (d + 1) * lanes]
         totals[pl.ds(d, nq, stride=2 * width), :] = jnp.where(low, a, pltpu.roll(b, half, 1))
         totals[pl.ds(width + d, nq, stride=2 * width), :] = jnp.where(low, pltpu.roll(a, half, 1), b)
-    out_ref[...] = totals[...].reshape(out_ref.shape).astype(BF)
-
-
-def right(recv, grad, width, inv_count, parts=8):
+    for r in range(2 * nq):
+        out_ref[r] = totals[pl.ds(pl.multiple_of(slots_ref[mine_ref[0], r] * width, width), width), :].astype(BF)
+
+
+def right(mine, slots, recv, grad, width, inv_count, parts=8):
     nq, tall, lanes = recv.shape
     depth, wide = grad.shape
     out = (2 * nq, width, lanes)
     return pl.pallas_call(
         functools.partial(right_kernel, inv_count, parts),
-        in_specs=[whole(recv.shape), pl.BlockSpec(memory_space=pl.ANY)],
+        in_specs=[pl.BlockSpec(memory_space=pltpu.SMEM)] * 2 + [whole(recv.shape), pl.BlockSpec(memory_space=pl.ANY)],
         out_specs=whole(out),
         grid=(1,),
         out_shape=jax.ShapeDtypeStruct(out, BF),
@@ -188,10 +190,10 @@
         compiler_params=params(BIG),
         cost_estimate=cost(8_000_000_000),
         name="right",
-    )(recv, grad)
-
-
-def left_kernel(inv_count, parts, recv_ref, grad_ref, rt_ref, out_ref, held, sems, spread, rows, totals):
+    )(mine, slots, recv, grad)
+
+
+def left_kernel(inv_count, parts, mine_ref, slots_ref, recv_ref, grad_ref, rt_ref, out_ref, held, sems, spread, rows, totals):
     nr, width, lanes = recv_ref.shape
     nq = nr // 2
     tall = out_ref.shape[1]
@@ -201,7 +203,8 @@
         return pltpu.make_async_copy(rows_of(grad_ref, index, count), rows_of(held, index, count), sems.at[index])
 
     lax.fori_loop(0, parts, lambda index, carry: copy(index).start(), None)
-    spread[...] = recv_ref[...].reshape(nr * width, lanes).astype(F32)
+    for r in range(nr):
+        spread[pl.ds(pl.multiple_of(slots_ref[mine_ref[0], r] * width, width), width), :] = recv_ref[r].astype(F32)
     low = low_lanes((nq, lanes), lanes // 2)
     for d in range(width):
         a = spread[pl.ds(d, nq, stride=2 * width), :]
@@ -226,14 +229,14 @@
     out_ref[...] = totals[...].reshape(out_ref.shape).astype(BF)
 
 
-def left(recv, grad, inv_count, parts=8):
+def left(mine, slots, recv, grad, inv_count, parts=8):
     nr, width, lanes = recv.shape
     nq = nr // 2
     deep, wide = grad.shape
     out = (nq, 2 * deep // lanes, lanes)
     return pl.pallas_call(
         functools.partial(left_kernel, inv_count, parts),
-        in_specs=[whole(recv.shape), pl.BlockSpec(memory_space=pl.ANY)],
+        in_specs=[pl.BlockSpec(memory_space=pltpu.SMEM)] * 2 + [whole(recv.shape), pl.BlockSpec(memory_space=pl.ANY)],
         out_specs=[whole((nr * width, lanes)), whole(out)],
         grid=(1,),
         out_shape=[jax.ShapeDtypeStruct((nr * width, lanes), BF), jax.ShapeDtypeStruct(out, BF)],
@@ -247,7 +250,7 @@
         compiler_params=params(BIG),
         cost_estimate=cost(8_000_000_000),
         name="left",
-    )(recv, grad)
+    )(mine, slots, recv, grad)
 
 
 def weight_kernel(inv_count, recv_ref, rt_ref, cot_ref, out_ref, rows_ref, spread, held, totals):
@@ -450,7 +453,7 @@
     return pl.pallas_call(
         align_kernel,
         grid=(1,),
-        in_specs=[whole(v.shape) for v in (left, right, x, factor, behind)],
+        in_specs=[whole(v.shape) for v in (left, right, x, factor)] + [pl.BlockSpec(memory_space=pl.ANY)],
         out_specs=whole(x.shape),
         out_shape=jax.ShapeDtypeStruct(x.shape, BF),
         scratch_shapes=[pltpu.VMEM((x.shape[0] * x.shape[1], LANES), F32)],
@@ -560,6 +563,38 @@
     return list(found.values())
 
 
+def ring(a, b, size):
+    return min((a - b) % size, (b - a) % size)
+
+
+def nearest(nq, side):
+    line = nq // 2
+    found = []
+    for q in range(nq):
+        x, y = q // side, q % side
+
+        def hops(s, t):
+            along_y = ring(s // line * side + y, q // line * side + t % side, 2 * side)
+            return ring(s % line, q % line, line) + along_y + ring(x, t // side, side)
+
+        for most in range(4 * nq):
+            held = {}
+
+            def place(s, seen):
+                for t in sorted(range(nq), key=lambda t: hops(s, t)):
+                    if hops(s, t) <= most and t not in seen:
+                        seen.add(t)
+                        if t not in held or place(held[t], seen):
+                            held[t] = s
+                            return True
+                return False
+
+            if all(place(s, set()) for s in range(nq)):
+                break
+        found.append([held[t] for t in range(nq)])
+    return found
+
+
 def body(nq, nr, homolog_matrix, factor_matrix, output_weight, output_bias, pairwise_cotangent):
     width = factor_matrix.shape[1] // 2
     inv_count = 1.0 / (2 * nq)
@@ -567,7 +602,12 @@
     line = nq // 2
     outer = grouped(pairs, nr, lambda a, b: (a % line, b % 2))
     inner = grouped(pairs, nr, lambda a, b: (a // line, b // 2))
-    there = [(s * nr + r, (r // 2) * nr + 2 * s + r % 2) for s in range(nq) for r in range(nr)]
+    senders = nearest(nq, 4)
+    halves = [(q, t, h) for q in range(nq) for t in range(nq) for h in range(2)]
+    there = [(senders[q][t] * nr + 2 * q + h, q * nr + 2 * t + h) for q, t, h in halves]
+    table = np.array([2 * senders[q][t] + h for q, t, h in halves], np.int32).reshape(nq, nr)
+    slots = jnp.asarray(table)
+    mine = lax.axis_index("seq").astype(jnp.int32).reshape(1)
     back = [(b, a) for a, b in there]
     bias = output_bias.reshape(1, -1)
     factor = factor_matrix.T
@@ -578,25 +618,24 @@
     right_moved = jnp.concatenate(jnp.split(tail, tail.shape[1] // LANES, axis=1), axis=0)
     grad, w = grad_outer(output_weight, pairwise_cotangent, width)
     right_all = exchange(jnp.broadcast_to(right_moved, (nr,) + right_moved.shape), "res")
-    right_in = exchange(right(left_all, grad, width, inv_count), "res")
-    rt, left_out = left(right_all, grad, inv_count)
+    right_in = exchange(right(mine, slots, left_all, grad, width, inv_count), "res")
+    rt, left_out = left(mine, slots, right_all, grad, inv_count)
     left_in = exchange(left_out, "seq")
     wo, rows = weight(left_all, rt, pairwise_cotangent, width, inv_count)
     right_total = total(right_in)
     payload = payload_of(left_in, right_total, packed, moved, wo)
     residues = pairwise_cotangent.shape[0]
     steps = residues // 8
-    cuts = [0, (steps + 2) // 3, (2 * steps + 2) // 3, steps]
+    cut = steps // 2
     summed = exchange_in(payload, outer)
-    pair, token = pair_part(rows, w, rt, bias, residues, cuts[0], cuts[1], payload)
-    payload = total_copies(summed, width, len(inner[0]), token)
+    right_back = lax.ppermute(hold(right_total, payload), ("seq", "res"), back)
+    payload = total_copies(summed, width, len(inner[0]), right_back)
     summed = exchange_in(payload, inner)
-    pair, token = pair_part(rows, w, rt, bias, residues, cuts[1], cuts[2], payload, pair)
+    pair, token = pair_part(rows, w, rt, bias, residues, 0, cut, payload)
     payload = total_copies(summed, width, len(outer[0]), token)
     summed = exchange_in(payload, outer)
-    right_back = lax.ppermute(hold(right_total, payload), ("seq", "res"), back)
-    pairwise_update, token = pair_part(rows, w, rt, bias, residues, cuts[2], cuts[3], payload, pair)
-    alignment_gradient = align(left_in, right_back, homolog_matrix, factor, token)
+    pairwise_update, _ = pair_part(rows, w, rt, bias, residues, cut, steps, payload, pair)
+    alignment_gradient = align(left_in, right_back, homolog_matrix, factor, payload)
     factor_grad, output_weight_gradient = last(summed, width, factor.shape)
     return (pairwise_update, alignment_gradient, factor_grad.T, output_weight_gradient)
 

time: 163 us -> 160 us (0.982); the launches traced: 160 us -> 159 us
  waiting for transfers between devices: 26.8 us -> 29.1 us
  Pallas kernels: 60.6 us -> 58.7 us
    all_to_all x3, waiting for transfers between devices: 20.8 us -> 23.1 us  [exchange_in(): lax.all_to_all(parts, ('seq', 'res'), 0, 0, axis_index_groups=groups, til...]
    pallas_call x3 -> x2, Pallas kernels: 14 us -> 12.1 us  [pair_part(): pl.pallas_call(pair_kernel, grid=(end - begin,), in_specs=[pl.BlockSpec((...]
  transfers between devices with their start and end apart: 9 -> 9, of which waited for: 6 -> 6; matrix products, arithmetic and copies ran while one was open for 1% -> 1% of each run, Pallas kernels for 34% -> 33%
where the time goes in v3:
time: 160 us; the launch traced here: 159 us
  starting transfers between devices  66.5 us (42%)
  Pallas kernels  58.7 us (37%)
  waiting for transfers between devices  29.1 us (18%)
  local copies, waits for them, and re-layouts  3.77 us (2%)
    all_to_all x4, starting transfers between devices, exchange(): return lax.all_to_all(parts, axis, 0, 0, tiled=True)  41.6 us
    all_to_all x3, waiting for transfers between devices, exchange_in(): lax.all_to_all(parts, ('seq', 'res'), 0, 0, axis_index_groups=groups, til...  23.1 us
    all_to_all x3, starting transfers between devices, exchange_in(): lax.all_to_all(parts, ('seq', 'res'), 0, 0, axis_index_groups=groups, til...  22.7 us
    pallas_call x2, Pallas kernels, pair_part(): pl.pallas_call(pair_kernel, grid=(end - begin,), in_specs=[pl.BlockSpec((...  12.1 us
    pallas_call x1, Pallas kernels, weight(): pl.pallas_call(functools.partial(weight_kernel, inv_count), grid=(residue...  12 us
    pallas_call x1, Pallas kernels, grad_outer(): pl.pallas_call(functools.partial(grad_outer_kernel, parts), in_specs=[who...  9.94 us
    pallas_call x1, Pallas kernels, left(): pl.pallas_call(functools.partial(left_kernel, inv_count, parts), in_specs...  9.31 us
    pallas_call x1, Pallas kernels, right(): pl.pallas_call(functools.partial(right_kernel, inv_count, parts), in_spec...  8.58 us
  transfers between devices with their start and end apart: 9, of which 6 were waited for; matrix products, arithmetic and copies ran while one was open for 1% of the time, Pallas kernels for 33%

profile of v3, /device:TPU:1, one launch (start us, length us, event | category | flops | bytes accessed | tf_op | source)
XLA Modules:
  0.0 158.8 jit_solution(18062165438900536151)
XLA Ops:
  0.6 1.8 %before.1 = (bf16[32,128]{1,0:T(8,128)(2,1)}, bf16[144,256]{1,0:T(8,128)(2,1)}) custom-call(bf16[2,64,256]{2,1,0:T(8,128)(2,1)} %x_ref.3, bf16[64,256]{1,0:T(8,128)(2,1)} %bitcast.4), custom_call_target="tpu_custom_call" | custom-call | tf_op jit(solution)/shard_map/before/pallas_call | solution.py:73
  2.5 1.5 collective-permute-start
  4.0 1.4 broadcast_in_dim.6
  5.4 16.6 %all-to-all-start = ((bf16[16,32,128]{2,1,0:T(8,128)(2,1)}), bf16[16,32,128]{2,1,0:T(8,128)(2,1)S(1)}, u32[]{:S(2)}, u32[]{:S(2)}) async-start(bf16[16,32,128]{2,1,0:T(8,128)(2,1)} %broadcast_in_dim.6), calls=%async_computation | async-start | bytes 262144 | tf_op jit(solution)/shard_map/all_to_all | solution.py:552
  22.0 9.9 %grad_outer.1 = (bf16[2048,4096]{1,0:T(8,128)(2,1)}, bf16[1024,128]{1,0:T(8,128)(2,1)}) custom-call(bf16[1024,128]{1,0:T(8,128)(2,1)} %given_ref.1, bf16[64,128,128]{2,1,0:T(8,128)(2,1)} %cot_ref.3), custom_call_target="tpu_custom_call" | custom-call | flops 8000000000 | bytes 4000000 | tf_op jit(solution)/shard_map/grad_outer/pallas_call | solution.py:125
  32.0 0.0 collective-permute-done.moved_ref
  32.0 1.3 all-to-all-done.recv_ref
  33.3 0.0 copy-start.6
  33.3 0.7 broadcast_in_dim.7
  34.1 10.7 %all-to-all-start.1 = ((bf16[32,32,128]{2,1,0:T(8,128)(2,1)}), bf16[32,32,128]{2,1,0:T(8,128)(2,1)S(1)}, u32[]{:S(2)}, u32[]{:S(2)}) async-start(bf16[32,32,128]{2,1,0:T(8,128)(2,1)} %broadcast_in_dim.7), calls=%async_computation.1 | async-start | bytes 524288 | tf_op jit(solution)/shard_map/all_to_all | solution.py:552
  44.7 0.0 copy-done.6
  44.8 8.6 %right.1 = bf16[32,32,128]{2,1,0:T(8,128)(2,1)} custom-call(s32[1]{0:T(128)} %bitcast.1.mine_ref, s32[16,32]{1,0:T(8,128)} %constant.8.clone.slots_ref, bf16[16,32,128]{2,1,0:T(8,128)(2,1)} %copy-done.6, bf16[2048,4096]{1,0:T(8,128)(2,1)} %get-tuple-element.19.grad_ref), custom_call_target="tpu_custom_call" | custom-call | flops 8000000000 | bytes 4000000 | tf_op jit(solution)/shard_map/right/pallas_call | solution.py:176
  53.3 2.7 %all-to-all-done.1.recv_ref = bf16[32,32,128]{2,1,0:T(8,128)(2,1)S(1)} async-done(((bf16[32,32,128]{2,1,0:T(8,128)(2,1)}), bf16[32,32,128]{2,1,0:T(8,128)(2,1)S(1)}, u32[]{:S(2)}, u32[]{:S(2)}) %all-to-all-start.1) | async-done | bytes 262176 | tf_op jit(solution)/shard_map/all_to_all | solution.py:552
  56.0 0.0 copy-start.5
  56.0 5.0 %all-to-all-start.3 = ((bf16[32,32,128]{2,1,0:T(8,128)(2,1)}), bf16[32,32,128]{2,1,0:T(8,128)(2,1)S(1)}, u32[]{:S(2)}, u32[]{:S(2)}) async-start(bf16[32,32,128]{2,1,0:T(8,128)(2,1)} %right.1), calls=%async_computation.3 | async-start | bytes 524288 | tf_op jit(solution)/shard_map/all_to_all | solution.py:552
  61.1 0.0 copy-done.5
  61.1 9.3 %left.1 = (bf16[1024,128]{1,0:T(8,128)(2,1)}, bf16[16,32,128]{2,1,0:T(8,128)(2,1)}) custom-call(s32[1]{0:T(128)} %bitcast.1.mine_ref, s32[16,32]{1,0:T(8,128)} %constant.8.clone.slots_ref, bf16[32,32,128]{2,1,0:T(8,128)(2,1)} %copy-done.5, bf16[2048,4096]{1,0:T(8,128)(2,1)} %get-tuple-element.19.grad_ref), custom_call_target="tpu_custom_call" | custom-call | flops 8000000000 | bytes 4000000 | tf_op jit(solution)/shard_map/left/pallas_call | solution.py:237
  70.4 2.0 %all-to-all-done.3.in_ref = bf16[32,32,128]{2,1,0:T(8,128)(2,1)S(1)} async-done(((bf16[32,32,128]{2,1,0:T(8,128)(2,1)}), bf16[32,32,128]{2,1,0:T(8,128)(2,1)S(1)}, u32[]{:S(2)}, u32[]{:S(2)}) %all-to-all-start.3) | async-done | bytes 262176 | tf_op jit(solution)/shard_map/all_to_all | solution.py:552
  72.4 9.3 %all-to-all-start.2 = ((bf16[16,32,128]{2,1,0:T(8,128)(2,1)}), bf16[16,32,128]{2,1,0:T(8,128)(2,1)S(1)}, u32[]{:S(2)}, u32[]{:S(2)}) async-start(bf16[16,32,128]{2,1,0:T(8,128)(2,1)} %get-tuple-element.23), calls=%async_computation.2 | async-start | bytes 262144 | tf_op jit(solution)/shard_map/all_to_all | solution.py:552
  81.6 0.0 copy-start.3
  81.6 12.0 %weight.1 = (bf16[32,32,128]{2,1,0:T(8,128)(2,1)}, bf16[2048,128]{1,0:T(8,128)(2,1)}) custom-call(bf16[16,32,128]{2,1,0:T(8,128)(2,1)} %copy-done.6, bf16[1024,128]{1,0:T(8,128)(2,1)} %get-tuple-element.20.rt_ref, bf16[64,128,128]{2,1,0:T(8,128)(2,1)} %cot_ref.3), custom_call_target="tpu_custom_call" | custom-call | flops 16000000000 | bytes 4000000 | tf_op jit(solution)/shard_map/weight/pallas_call | solution.py:319
  93.6 0.1 total.1.right_ref.in_ref
  93.7 0.0 all-to-all-done.2.left_ref
  93.7 0.0 copy-done.3
  93.7 0.0 copy-start
  93.7 0.9 copy-done
  94.7 1.0 payload.1.behind_ref
  95.7 7.7 %all-to-all-start.4 = ((bf16[32,40,128]{2,1,0:T(8,128)(2,1)}), bf16[32,40,128]{2,1,0:T(8,128)(2,1)S(1)}, u32[]{:S(2)}, u32[]{:S(2)}) async-start(bf16[32,40,128]{2,1,0:T(8,128)(2,1)} %payload.1.behind_ref), calls=%async_computation.4 | async-start | bytes 655360 | tf_op jit(solution)/shard_map/all_to_all | solution.py:556
  103.4 0.7 collective-permute-start.1
  104.1 0.0 collective-permute-done.1.behind_ref.right_ref
  104.1 12.1 %all-to-all-done.4.in_ref = bf16[32,40,128]{2,1,0:T(8,128)(2,1)S(1)} async-done(((bf16[32,40,128]{2,1,0:T(8,128)(2,1)}), bf16[32,40,128]{2,1,0:T(8,128)(2,1)S(1)}, u32[]{:S(2)}, u32[]{:S(2)}) %all-to-all-start.4) | async-done | bytes 327712 | tf_op jit(solution)/shard_map/all_to_all | solution.py:556
  116.2 0.7 total_copies.2.refs_0_
  116.9 9.3 %all-to-all-start.5 = ((bf16[16,40,128]{2,1,0:T(8,128)(2,1)}), bf16[16,40,128]{2,1,0:T(8,128)(2,1)S(1)}, u32[]{:S(2)}, u32[]{:S(2)}) async-start(bf16[16,40,128]{2,1,0:T(8,128)(2,1)} %total_copies.2.refs_0_), calls=%async_computation.5 | async-start | bytes 327680 | tf_op jit(solution)/shard_map/all_to_all | solution.py:556
  126.2 0.0 copy-start.1
  126.2 0.0 copy-start.2
  126.2 6.1 %pair_part.2 = (bf16[64,128,128]{2,1,0:T(8,128)(2,1)}, f32[8,128]{1,0:T(8,128)}) custom-call(bf16[2048,128]{1,0:T(8,128)(2,1)} %get-tuple-element.21.rows_ref, bf16[1024,128]{1,0:T(8,128)(2,1)} %get-tuple-element.22.w_ref, bf16[1024,128]{1,0:T(8,128)(2,1)} %get-tuple-element.20.rt_ref, f32[1,128]{1,0:T(1,128)} %bitcast.7, ...), custom_call_target="tpu_custom_call" | custom-call | flops 6000000000 | bytes 4000000 | tf_op jit(solution)/shard_map/pair_part/pallas_call | solution.py:374
  132.3 3.6 %all-to-all-done.5.in_ref = bf16[16,40,128]{2,1,0:T(8,128)(2,1)S(1)} async-done(((bf16[16,40,128]{2,1,0:T(8,128)(2,1)}), bf16[16,40,128]{2,1,0:T(8,128)(2,1)S(1)}, u32[]{:S(2)}, u32[]{:S(2)}) %all-to-all-start.5) | async-done | bytes 163872 | tf_op jit(solution)/shard_map/all_to_all | solution.py:556
  135.9 0.0 copy-start.4
  135.9 0.7 copy-done.4
  136.6 0.8 total_copies.3.refs_0_.behind_ref
  137.3 5.7 %all-to-all-start.6 = ((bf16[32,40,128]{2,1,0:T(8,128)(2,1)}), bf16[32,40,128]{2,1,0:T(8,128)(2,1)S(1)}, u32[]{:S(2)}, u32[]{:S(2)}) async-start(bf16[32,40,128]{2,1,0:T(8,128)(2,1)} %total_copies.3.refs_0_.behind_ref), calls=%async_computation.6 | async-start | bytes 655360 | tf_op jit(solution)/shard_map/all_to_all | solution.py:556
  143.1 0.0 copy-done.1
  143.1 0.0 copy-done.2
  143.1 1.0 align.1
  144.1 6.0 %pair_part.3 = (bf16[64,128,128]{2,1,0:T(8,128)(2,1)}, f32[8,128]{1,0:T(8,128)}) custom-call(bf16[2048,128]{1,0:T(8,128)(2,1)} %get-tuple-element.21.rows_ref, bf16[1024,128]{1,0:T(8,128)(2,1)} %get-tuple-element.22.w_ref, bf16[1024,128]{1,0:T(8,128)(2,1)} %get-tuple-element.20.rt_ref, f32[1,128]{1,0:T(1,128)} %bitcast.8, ...), custom_call_target="tpu_custom_call", output_to_operand_aliasing={{0}: (5, {})} | custom-call | flops 6000000000 | bytes 4000000 | tf_op jit(solution)/shard_map/pair_part/pallas_call | solution.py:374
  150.1 7.4 %all-to-all-done.6.in_ref = bf16[32,40,128]{2,1,0:T(8,128)(2,1)S(1)} async-done(((bf16[32,40,128]{2,1,0:T(8,128)(2,1)}), bf16[32,40,128]{2,1,0:T(8,128)(2,1)S(1)}, u32[]{:S(2)}, u32[]{:S(2)}) %all-to-all-start.6) | async-done | bytes 327712 | tf_op jit(solution)/shard_map/all_to_all | solution.py:556
  157.5 1.3 last.1
  (3 shorter events, 0.0 us)
Async XLA Ops:
  2.5 29.5 %collective-permute-start = (bf16[144,256]{1,0:T(8,128)(2,1)}, bf16[144,256]{1,0:T(8,128)(2,1)S(1)}, u32[]{:S(2)}, u32[]{:S(2)}) collective-permute-start(bf16[144,256]{1,0:T(8,128)(2,1)} %get-tuple-element.18.normed_ref), channel_id=1, source_target_pairs={{0,0},{1,1},{448,2},{449,3},{480,4},{481,5},{384,6},{385,7},{32,8}... | collective-permute-start | bytes 221192 | tf_op jit(solution)/shard_map/ppermute | solution.py:615
  5.4 28.0 %all-to-all-start = ((bf16[16,32,128]{2,1,0:T(8,128)(2,1)}), bf16[16,32,128]{2,1,0:T(8,128)(2,1)S(1)}, u32[]{:S(2)}, u32[]{:S(2)}) async-start(bf16[16,32,128]{2,1,0:T(8,128)(2,1)} %broadcast_in_dim.6), calls=%async_computation | async-start | bytes 262144 | tf_op jit(solution)/shard_map/all_to_all | solution.py:552
  33.3 11.4 %copy-start.6 = (bf16[16,32,128]{2,1,0:T(8,128)(2,1)}, bf16[16,32,128]{2,1,0:T(8,128)(2,1)S(1)}, u32[]{:S(2)}) copy-start(bf16[16,32,128]{2,1,0:T(8,128)(2,1)S(1)} %all-to-all-done.recv_ref) | copy-start | bytes 393220
  34.1 21.9 %all-to-all-start.1 = ((bf16[32,32,128]{2,1,0:T(8,128)(2,1)}), bf16[32,32,128]{2,1,0:T(8,128)(2,1)S(1)}, u32[]{:S(2)}, u32[]{:S(2)}) async-start(bf16[32,32,128]{2,1,0:T(8,128)(2,1)} %broadcast_in_dim.7), calls=%async_computation.1 | async-start | bytes 524288 | tf_op jit(solution)/shard_map/all_to_all | solution.py:552
  56.0 5.1 %copy-start.5 = (bf16[32,32,128]{2,1,0:T(8,128)(2,1)}, bf16[32,32,128]{2,1,0:T(8,128)(2,1)S(1)}, u32[]{:S(2)}) copy-start(bf16[32,32,128]{2,1,0:T(8,128)(2,1)S(1)} %all-to-all-done.1.recv_ref) | copy-start | bytes 786436
  56.0 16.3 %all-to-all-start.3 = ((bf16[32,32,128]{2,1,0:T(8,128)(2,1)}), bf16[32,32,128]{2,1,0:T(8,128)(2,1)S(1)}, u32[]{:S(2)}, u32[]{:S(2)}) async-start(bf16[32,32,128]{2,1,0:T(8,128)(2,1)} %right.1), calls=%async_computation.3 | async-start | bytes 524288 | tf_op jit(solution)/shard_map/all_to_all | solution.py:552
  72.4 21.3 %all-to-all-start.2 = ((bf16[16,32,128]{2,1,0:T(8,128)(2,1)}), bf16[16,32,128]{2,1,0:T(8,128)(2,1)S(1)}, u32[]{:S(2)}, u32[]{:S(2)}) async-start(bf16[16,32,128]{2,1,0:T(8,128)(2,1)} %get-tuple-element.23), calls=%async_computation.2 | async-start | bytes 262144 | tf_op jit(solution)/shard_map/all_to_all | solution.py:552
  81.6 12.1 %copy-start.3 = (bf16[144,256]{1,0:T(8,128)(2,1)S(1)}, bf16[144,256]{1,0:T(8,128)(2,1)}, u32[]{:S(2)}) copy-start(bf16[144,256]{1,0:T(8,128)(2,1)} %get-tuple-element.18.normed_ref) | copy-start | bytes 221188
  93.7 1.0 copy-start
  95.7 20.5 %all-to-all-start.4 = ((bf16[32,40,128]{2,1,0:T(8,128)(2,1)}), bf16[32,40,128]{2,1,0:T(8,128)(2,1)S(1)}, u32[]{:S(2)}, u32[]{:S(2)}) async-start(bf16[32,40,128]{2,1,0:T(8,128)(2,1)} %payload.1.behind_ref), calls=%async_computation.4 | async-start | bytes 655360 | tf_op jit(solution)/shard_map/all_to_all | solution.py:556
  103.4 0.7 collective-permute-start.1
  116.9 18.9 %all-to-all-start.5 = ((bf16[16,40,128]{2,1,0:T(8,128)(2,1)}), bf16[16,40,128]{2,1,0:T(8,128)(2,1)S(1)}, u32[]{:S(2)}, u32[]{:S(2)}) async-start(bf16[16,40,128]{2,1,0:T(8,128)(2,1)} %total_copies.2.refs_0_), calls=%async_computation.5 | async-start | bytes 327680 | tf_op jit(solution)/shard_map/all_to_all | solution.py:556
  126.2 16.8 %copy-start.1 = (bf16[2,64,256]{2,1,0:T(8,128)(2,1)S(1)}, bf16[2,64,256]{2,1,0:T(8,128)(2,1)}, u32[]{:S(2)}) copy-start(bf16[2,64,256]{2,1,0:T(8,128)(2,1)} %x_ref.3) | copy-start | bytes 196612
  126.2 16.8 %copy-start.2 = (bf16[256,64]{0,1:T(8,128)(2,1)S(1)}, bf16[256,64]{0,1:T(8,128)(2,1)}, u32[]{:S(2)}) copy-start(bf16[256,64]{0,1:T(8,128)(2,1)} %param.7) | copy-start | bytes 98308
  135.9 0.7 copy-start.4
  137.3 20.2 %all-to-all-start.6 = ((bf16[32,40,128]{2,1,0:T(8,128)(2,1)}), bf16[32,40,128]{2,1,0:T(8,128)(2,1)S(1)}, u32[]{:S(2)}, u32[]{:S(2)}) async-start(bf16[32,40,128]{2,1,0:T(8,128)(2,1)} %total_copies.3.refs_0_.behind_ref), calls=%async_computation.6 | async-start | bytes 655360 | tf_op jit(solution)/shard_map/all_to_all | solution.py:556

commit v4 on v3

--- a/solution.py
+++ b/solution.py
@@ -388,7 +388,7 @@
         ],
         scratch_shapes=[pltpu.VMEM((cols, depth), BF), pltpu.VMEM((depth, block * ch), BF)],
         input_output_aliases={} if held is None else {5: 0},
-        compiler_params=params(BIG),
+        compiler_params=params(40),
         cost_estimate=cost(6_000_000_000),
         name="pair_part",
     )(rows, w, rt, bias, *more)

time: 160 us -> 159 us (level)
  Pallas kernels: 58.7 us -> 56.5 us
  waiting for transfers between devices: 29.1 us -> 31.2 us
    pallas_call x2, Pallas kernels: 12.1 us -> 9.95 us  [pair_part(): pl.pallas_call(pair_kernel, grid=(end - begin,), in_specs=[pl.BlockSpec((...]
    all_to_all x3, waiting for transfers between devices: 23.1 us -> 25.2 us  [exchange_in(): lax.all_to_all(parts, ('seq', 'res'), 0, 0, axis_index_groups=groups, til...]
  transfers between devices with their start and end apart: 9 -> 9, of which waited for: 6 -> 6; matrix products, arithmetic and copies ran while one was open for 1% -> 1% of each run, Pallas kernels for 33% -> 32%
where the time goes in v4:
time: 159 us; the launch traced here: 158 us
  starting transfers between devices  66.4 us (42%)
  Pallas kernels  56.5 us (36%)
  waiting for transfers between devices  31.2 us (20%)
  local copies, waits for them, and re-layouts  3.13 us (2%)
    all_to_all x4, starting transfers between devices, exchange(): return lax.all_to_all(parts, axis, 0, 0, tiled=True)  41.6 us
    all_to_all x3, waiting for transfers between devices, exchange_in(): lax.all_to_all(parts, ('seq', 'res'), 0, 0, axis_index_groups=groups, til...  25.2 us
    all_to_all x3, starting transfers between devices, exchange_in(): lax.all_to_all(parts, ('seq', 'res'), 0, 0, axis_index_groups=groups, til...  22.7 us
    pallas_call x1, Pallas kernels, weight(): pl.pallas_call(functools.partial(weight_kernel, inv_count), grid=(residue...  12 us
    pallas_call x2, Pallas kernels, pair_part(): pl.pallas_call(pair_kernel, grid=(end - begin,), in_specs=[pl.BlockSpec((...  9.95 us
    pallas_call x1, Pallas kernels, grad_outer(): pl.pallas_call(functools.partial(grad_outer_kernel, parts), in_specs=[who...  9.89 us
    pallas_call x1, Pallas kernels, left(): pl.pallas_call(functools.partial(left_kernel, inv_count, parts), in_specs...  9.31 us
    pallas_call x1, Pallas kernels, right(): pl.pallas_call(functools.partial(right_kernel, inv_count, parts), in_spec...  8.58 us
  transfers between devices with their start and end apart: 9, of which 6 were waited for; matrix products, arithmetic and copies ran while one was open for 1% of the time, Pallas kernels for 32%

profile of v4, /device:TPU:1, one launch (start us, length us, event | category | flops | bytes accessed | tf_op | source)
XLA Modules:
  0.0 158.2 jit_solution(5433375183845342257)
XLA Ops:
  0.6 1.9 %before.1 = (bf16[32,128]{1,0:T(8,128)(2,1)}, bf16[144,256]{1,0:T(8,128)(2,1)}) custom-call(bf16[2,64,256]{2,1,0:T(8,128)(2,1)} %x_ref.3, bf16[64,256]{1,0:T(8,128)(2,1)} %bitcast.4), custom_call_target="tpu_custom_call" | custom-call | tf_op jit(solution)/shard_map/before/pallas_call | solution.py:73
  2.5 1.5 collective-permute-start
  4.0 1.4 broadcast_in_dim.6
  5.4 16.6 %all-to-all-start = ((bf16[16,32,128]{2,1,0:T(8,128)(2,1)}), bf16[16,32,128]{2,1,0:T(8,128)(2,1)S(1)}, u32[]{:S(2)}, u32[]{:S(2)}) async-start(bf16[16,32,128]{2,1,0:T(8,128)(2,1)} %broadcast_in_dim.6), calls=%async_computation | async-start | bytes 262144 | tf_op jit(solution)/shard_map/all_to_all | solution.py:552
  22.0 9.9 %grad_outer.1 = (bf16[2048,4096]{1,0:T(8,128)(2,1)}, bf16[1024,128]{1,0:T(8,128)(2,1)}) custom-call(bf16[1024,128]{1,0:T(8,128)(2,1)} %given_ref.1, bf16[64,128,128]{2,1,0:T(8,128)(2,1)} %cot_ref.3), custom_call_target="tpu_custom_call" | custom-call | flops 8000000000 | bytes 4000000 | tf_op jit(solution)/shard_map/grad_outer/pallas_call | solution.py:125
  31.9 0.0 collective-permute-done.moved_ref
  31.9 1.4 all-to-all-done.recv_ref
  33.3 0.7 broadcast_in_dim.7
  34.1 10.7 %all-to-all-start.1 = ((bf16[32,32,128]{2,1,0:T(8,128)(2,1)}), bf16[32,32,128]{2,1,0:T(8,128)(2,1)S(1)}, u32[]{:S(2)}, u32[]{:S(2)}) async-start(bf16[32,32,128]{2,1,0:T(8,128)(2,1)} %broadcast_in_dim.7), calls=%async_computation.1 | async-start | bytes 524288 | tf_op jit(solution)/shard_map/all_to_all | solution.py:552
  44.8 0.0 copy-done.9
  44.8 8.6 %right.1 = bf16[32,32,128]{2,1,0:T(8,128)(2,1)} custom-call(s32[1]{0:T(128)} %bitcast.1.mine_ref, s32[16,32]{1,0:T(8,128)} %constant.8.clone.slots_ref, bf16[16,32,128]{2,1,0:T(8,128)(2,1)} %copy-done.9, bf16[2048,4096]{1,0:T(8,128)(2,1)} %get-tuple-element.19.grad_ref), custom_call_target="tpu_custom_call" | custom-call | flops 8000000000 | bytes 4000000 | tf_op jit(solution)/shard_map/right/pallas_call | solution.py:176
  53.4 2.7 %all-to-all-done.1.recv_ref = bf16[32,32,128]{2,1,0:T(8,128)(2,1)S(1)} async-done(((bf16[32,32,128]{2,1,0:T(8,128)(2,1)}), bf16[32,32,128]{2,1,0:T(8,128)(2,1)S(1)}, u32[]{:S(2)}, u32[]{:S(2)}) %all-to-all-start.1) | async-done | bytes 262176 | tf_op jit(solution)/shard_map/all_to_all | solution.py:552
  56.0 5.0 %all-to-all-start.3 = ((bf16[32,32,128]{2,1,0:T(8,128)(2,1)}), bf16[32,32,128]{2,1,0:T(8,128)(2,1)S(1)}, u32[]{:S(2)}, u32[]{:S(2)}) async-start(bf16[32,32,128]{2,1,0:T(8,128)(2,1)} %right.1), calls=%async_computation.3 | async-start | bytes 524288 | tf_op jit(solution)/shard_map/all_to_all | solution.py:552
  61.1 0.0 copy-done.8
  61.1 9.3 %left.1 = (bf16[1024,128]{1,0:T(8,128)(2,1)}, bf16[16,32,128]{2,1,0:T(8,128)(2,1)}) custom-call(s32[1]{0:T(128)} %bitcast.1.mine_ref, s32[16,32]{1,0:T(8,128)} %constant.8.clone.slots_ref, bf16[32,32,128]{2,1,0:T(8,128)(2,1)} %copy-done.8, bf16[2048,4096]{1,0:T(8,128)(2,1)} %get-tuple-element.19.grad_ref), custom_call_target="tpu_custom_call" | custom-call | flops 8000000000 | bytes 4000000 | tf_op jit(solution)/shard_map/left/pallas_call | solution.py:237
  70.4 1.9 %all-to-all-done.3.in_ref = bf16[32,32,128]{2,1,0:T(8,128)(2,1)S(1)} async-done(((bf16[32,32,128]{2,1,0:T(8,128)(2,1)}), bf16[32,32,128]{2,1,0:T(8,128)(2,1)S(1)}, u32[]{:S(2)}, u32[]{:S(2)}) %all-to-all-start.3) | async-done | bytes 262176 | tf_op jit(solution)/shard_map/all_to_all | solution.py:552
  72.4 9.2 %all-to-all-start.2 = ((bf16[16,32,128]{2,1,0:T(8,128)(2,1)}), bf16[16,32,128]{2,1,0:T(8,128)(2,1)S(1)}, u32[]{:S(2)}, u32[]{:S(2)}) async-start(bf16[16,32,128]{2,1,0:T(8,128)(2,1)} %get-tuple-element.23), calls=%async_computation.2 | async-start | bytes 262144 | tf_op jit(solution)/shard_map/all_to_all | solution.py:552
  81.6 0.0 copy-start.3
  81.6 0.0 copy-start.7
  81.6 12.0 %weight.1 = (bf16[32,32,128]{2,1,0:T(8,128)(2,1)}, bf16[2048,128]{1,0:T(8,128)(2,1)}) custom-call(bf16[16,32,128]{2,1,0:T(8,128)(2,1)} %copy-done.9, bf16[1024,128]{1,0:T(8,128)(2,1)} %get-tuple-element.20.rt_ref, bf16[64,128,128]{2,1,0:T(8,128)(2,1)} %cot_ref.3), custom_call_target="tpu_custom_call" | custom-call | flops 16000000000 | bytes 4000000 | tf_op jit(solution)/shard_map/weight/pallas_call | solution.py:319
  93.7 0.1 total.1.right_ref.in_ref
  93.7 0.0 all-to-all-done.2.left_ref
  93.7 0.0 copy-done.3
  93.7 0.0 copy-start
  93.7 1.0 copy-done
  94.7 1.0 payload.1.behind_ref
  95.7 7.7 %all-to-all-start.4 = ((bf16[32,40,128]{2,1,0:T(8,128)(2,1)}), bf16[32,40,128]{2,1,0:T(8,128)(2,1)S(1)}, u32[]{:S(2)}, u32[]{:S(2)}) async-start(bf16[32,40,128]{2,1,0:T(8,128)(2,1)} %payload.1.behind_ref), calls=%async_computation.4 | async-start | bytes 655360 | tf_op jit(solution)/shard_map/all_to_all | solution.py:556
  103.4 0.7 collective-permute-start.1
  104.1 0.0 collective-permute-done.1.behind_ref.right_ref
  104.1 12.1 %all-to-all-done.4.in_ref = bf16[32,40,128]{2,1,0:T(8,128)(2,1)S(1)} async-done(((bf16[32,40,128]{2,1,0:T(8,128)(2,1)}), bf16[32,40,128]{2,1,0:T(8,128)(2,1)S(1)}, u32[]{:S(2)}, u32[]{:S(2)}) %all-to-all-start.4) | async-done | bytes 327712 | tf_op jit(solution)/shard_map/all_to_all | solution.py:556
  116.2 0.7 total_copies.2.refs_0_
  117.0 9.3 %all-to-all-start.5 = ((bf16[16,40,128]{2,1,0:T(8,128)(2,1)}), bf16[16,40,128]{2,1,0:T(8,128)(2,1)S(1)}, u32[]{:S(2)}, u32[]{:S(2)}) async-start(bf16[16,40,128]{2,1,0:T(8,128)(2,1)} %total_copies.2.refs_0_), calls=%async_computation.5 | async-start | bytes 327680 | tf_op jit(solution)/shard_map/all_to_all | solution.py:556
  126.3 0.0 copy-done.7
  126.3 0.0 copy-done.4
  126.3 0.0 copy-done.5
  126.3 0.0 copy-done.6
  126.3 0.0 copy-start.1
  126.3 0.0 copy-start.2
  126.3 5.0 %pair_part.2 = (bf16[64,128,128]{2,1,0:T(8,128)(2,1)}, f32[8,128]{1,0:T(8,128)S(1)}) custom-call(bf16[2048,128]{1,0:T(8,128)(2,1)S(1)} %copy-done.6, bf16[1024,128]{1,0:T(8,128)(2,1)S(1)} %copy-done.7, bf16[1024,128]{1,0:T(8,128)(2,1)S(1)} %copy-done.5, f32[1,128]{1,0:T(1,128)S(1)} %bitcast.6, bf16[16,40,128]{2,1,0:T(8,128)(2,1)} %total_copies.2.refs_0_), custom_call_target="tpu_custom_call" | custom-call | flops 6000000000 | bytes 4000000 | tf_op jit(solution)/shard_map/pair_part/pallas_call | solution.py:374
  131.3 4.6 %all-to-all-done.5.in_ref = bf16[16,40,128]{2,1,0:T(8,128)(2,1)S(1)} async-done(((bf16[16,40,128]{2,1,0:T(8,128)(2,1)}), bf16[16,40,128]{2,1,0:T(8,128)(2,1)S(1)}, u32[]{:S(2)}, u32[]{:S(2)}) %all-to-all-start.5) | async-done | bytes 163872 | tf_op jit(solution)/shard_map/all_to_all | solution.py:556
  135.9 0.8 total_copies.3.refs_0_.behind_ref
  136.7 5.7 %all-to-all-start.6 = ((bf16[32,40,128]{2,1,0:T(8,128)(2,1)}), bf16[32,40,128]{2,1,0:T(8,128)(2,1)S(1)}, u32[]{:S(2)}, u32[]{:S(2)}) async-start(bf16[32,40,128]{2,1,0:T(8,128)(2,1)} %total_copies.3.refs_0_.behind_ref), calls=%async_computation.6 | async-start | bytes 655360 | tf_op jit(solution)/shard_map/all_to_all | solution.py:556
  142.4 0.0 copy-done.1
  142.4 0.0 copy-done.2
  142.4 1.0 align.1
  143.4 5.0 %pair_part.3 = (bf16[64,128,128]{2,1,0:T(8,128)(2,1)}, f32[8,128]{1,0:T(8,128)}) custom-call(bf16[2048,128]{1,0:T(8,128)(2,1)S(1)} %copy-done.6, bf16[1024,128]{1,0:T(8,128)(2,1)S(1)} %copy-done.7, bf16[1024,128]{1,0:T(8,128)(2,1)S(1)} %copy-done.5, f32[1,128]{1,0:T(1,128)S(1)} %bitcast.7, ...), custom_call_target="tpu_custom_call", output_to_operand_aliasing={{0}: (5, {})} | custom-call | flops 6000000000 | bytes 4000000 | tf_op jit(solution)/shard_map/pair_part/pallas_call | solution.py:374
  148.4 8.5 %all-to-all-done.6.in_ref = bf16[32,40,128]{2,1,0:T(8,128)(2,1)S(1)} async-done(((bf16[32,40,128]{2,1,0:T(8,128)(2,1)}), bf16[32,40,128]{2,1,0:T(8,128)(2,1)S(1)}, u32[]{:S(2)}, u32[]{:S(2)}) %all-to-all-start.6) | async-done | bytes 327712 | tf_op jit(solution)/shard_map/all_to_all | solution.py:556
  156.9 1.3 last.1
  (8 shorter events, 0.0 us)
Async XLA Ops:
  2.5 29.4 %collective-permute-start = (bf16[144,256]{1,0:T(8,128)(2,1)}, bf16[144,256]{1,0:T(8,128)(2,1)S(1)}, u32[]{:S(2)}, u32[]{:S(2)}) collective-permute-start(bf16[144,256]{1,0:T(8,128)(2,1)} %get-tuple-element.18.normed_ref), channel_id=1, source_target_pairs={{0,0},{1,1},{448,2},{449,3},{480,4},{481,5},{384,6},{385,7},{32,8}... | collective-permute-start | bytes 221192 | tf_op jit(solution)/shard_map/ppermute | solution.py:615
  5.4 28.0 %all-to-all-start = ((bf16[16,32,128]{2,1,0:T(8,128)(2,1)}), bf16[16,32,128]{2,1,0:T(8,128)(2,1)S(1)}, u32[]{:S(2)}, u32[]{:S(2)}) async-start(bf16[16,32,128]{2,1,0:T(8,128)(2,1)} %broadcast_in_dim.6), calls=%async_computation | async-start | bytes 262144 | tf_op jit(solution)/shard_map/all_to_all | solution.py:552
  33.3 11.4 %copy-start.9 = (bf16[16,32,128]{2,1,0:T(8,128)(2,1)}, bf16[16,32,128]{2,1,0:T(8,128)(2,1)S(1)}, u32[]{:S(2)}) copy-start(bf16[16,32,128]{2,1,0:T(8,128)(2,1)S(1)} %all-to-all-done.recv_ref) | copy-start | bytes 393220
  34.1 21.9 %all-to-all-start.1 = ((bf16[32,32,128]{2,1,0:T(8,128)(2,1)}), bf16[32,32,128]{2,1,0:T(8,128)(2,1)S(1)}, u32[]{:S(2)}, u32[]{:S(2)}) async-start(bf16[32,32,128]{2,1,0:T(8,128)(2,1)} %broadcast_in_dim.7), calls=%async_computation.1 | async-start | bytes 524288 | tf_op jit(solution)/shard_map/all_to_all | solution.py:552
  56.0 5.1 %copy-start.8 = (bf16[32,32,128]{2,1,0:T(8,128)(2,1)}, bf16[32,32,128]{2,1,0:T(8,128)(2,1)S(1)}, u32[]{:S(2)}) copy-start(bf16[32,32,128]{2,1,0:T(8,128)(2,1)S(1)} %all-to-all-done.1.recv_ref) | copy-start | bytes 786436
  56.0 16.3 %all-to-all-start.3 = ((bf16[32,32,128]{2,1,0:T(8,128)(2,1)}), bf16[32,32,128]{2,1,0:T(8,128)(2,1)S(1)}, u32[]{:S(2)}, u32[]{:S(2)}) async-start(bf16[32,32,128]{2,1,0:T(8,128)(2,1)} %right.1), calls=%async_computation.3 | async-start | bytes 524288 | tf_op jit(solution)/shard_map/all_to_all | solution.py:552
  72.4 21.3 %all-to-all-start.2 = ((bf16[16,32,128]{2,1,0:T(8,128)(2,1)}), bf16[16,32,128]{2,1,0:T(8,128)(2,1)S(1)}, u32[]{:S(2)}, u32[]{:S(2)}) async-start(bf16[16,32,128]{2,1,0:T(8,128)(2,1)} %get-tuple-element.23), calls=%async_computation.2 | async-start | bytes 262144 | tf_op jit(solution)/shard_map/all_to_all | solution.py:552
  81.6 12.1 %copy-start.3 = (bf16[144,256]{1,0:T(8,128)(2,1)S(1)}, bf16[144,256]{1,0:T(8,128)(2,1)}, u32[]{:S(2)}) copy-start(bf16[144,256]{1,0:T(8,128)(2,1)} %get-tuple-element.18.normed_ref) | copy-start | bytes 221188
  81.6 44.6 %copy-start.7 = (bf16[1024,128]{1,0:T(8,128)(2,1)S(1)}, bf16[1024,128]{1,0:T(8,128)(2,1)}, u32[]{:S(2)}) copy-start(bf16[1024,128]{1,0:T(8,128)(2,1)} %get-tuple-element.22.w_ref) | copy-start | bytes 786436
  93.7 32.6 %copy-start.4 = (f32[128]{0:T(128)S(1)}, f32[128]{0:T(128)}, u32[]{:S(2)}) copy-start(f32[128]{0:T(128)} %param.9) | copy-start | bytes 1540
  93.7 32.6 %copy-start.5 = (bf16[1024,128]{1,0:T(8,128)(2,1)S(1)}, bf16[1024,128]{1,0:T(8,128)(2,1)}, u32[]{:S(2)}) copy-start(bf16[1024,128]{1,0:T(8,128)(2,1)} %get-tuple-element.20.rt_ref) | copy-start | bytes 786436
  93.7 1.0 copy-start
  94.7 31.6 %copy-start.6 = (bf16[2048,128]{1,0:T(8,128)(2,1)S(1)}, bf16[2048,128]{1,0:T(8,128)(2,1)}, u32[]{:S(2)}) copy-start(bf16[2048,128]{1,0:T(8,128)(2,1)} %get-tuple-element.21.rows_ref) | copy-start | bytes 1572868
  95.7 20.5 %all-to-all-start.4 = ((bf16[32,40,128]{2,1,0:T(8,128)(2,1)}), bf16[32,40,128]{2,1,0:T(8,128)(2,1)S(1)}, u32[]{:S(2)}, u32[]{:S(2)}) async-start(bf16[32,40,128]{2,1,0:T(8,128)(2,1)} %payload.1.behind_ref), calls=%async_computation.4 | async-start | bytes 655360 | tf_op jit(solution)/shard_map/all_to_all | solution.py:556
  103.4 0.7 collective-permute-start.1
  117.0 19.0 %all-to-all-start.5 = ((bf16[16,40,128]{2,1,0:T(8,128)(2,1)}), bf16[16,40,128]{2,1,0:T(8,128)(2,1)S(1)}, u32[]{:S(2)}, u32[]{:S(2)}) async-start(bf16[16,40,128]{2,1,0:T(8,128)(2,1)} %total_copies.2.refs_0_), calls=%async_computation.5 | async-start | bytes 327680 | tf_op jit(solution)/shard_map/all_to_all | solution.py:556
  126.3 16.1 %copy-start.1 = (bf16[2,64,256]{2,1,0:T(8,128)(2,1)S(1)}, bf16[2,64,256]{2,1,0:T(8,128)(2,1)}, u32[]{:S(2)}) copy-start(bf16[2,64,256]{2,1,0:T(8,128)(2,1)} %x_ref.3) | copy-start | bytes 196612
  126.3 16.1 %copy-start.2 = (bf16[256,64]{0,1:T(8,128)(2,1)S(1)}, bf16[256,64]{0,1:T(8,128)(2,1)}, u32[]{:S(2)}) copy-start(bf16[256,64]{0,1:T(8,128)(2,1)} %param.7) | copy-start | bytes 98308
  136.7 20.2 %all-to-all-start.6 = ((bf16[32,40,128]{2,1,0:T(8,128)(2,1)}), bf16[32,40,128]{2,1,0:T(8,128)(2,1)S(1)}, u32[]{:S(2)}, u32[]{:S(2)}) async-start(bf16[32,40,128]{2,1,0:T(8,128)(2,1)} %total_copies.3.refs_0_.behind_ref), calls=%async_computation.6 | async-start | bytes 655360 | tf_op jit(solution)/shard_map/all_to_all | solution.py:556

commit v5 on v4

--- a/solution.py
+++ b/solution.py
@@ -429,7 +429,7 @@
         payload_kernel,
         out_shape=jax.ShapeDtypeStruct((chunks, width + extra, lanes), BF),
         scratch_shapes=[pltpu.VMEM((rows, LANES), F32)],
-        compiler_params=params(),
+        compiler_params=params(BIG),
         name="payload",
     )(left, right, normed, moved, wo)
 

time: 159 us -> 162 us (1.019)
  local copies, waits for them, and re-layouts: 3.13 us -> 5.13 us
  waiting for transfers between devices: 31.2 us -> 29.5 us
  starting transfers between devices: 66.4 us -> 68.1 us
    unnamed x20 -> x28, local copies, waits for them, and re-layouts: 1.02 us -> 3.01 us
    all_to_all x3, waiting for transfers between devices: 25.2 us -> 23.5 us  [exchange_in(): lax.all_to_all(parts, ('seq', 'res'), 0, 0, axis_index_groups=groups, til...]
    all_to_all x3, starting transfers between devices: 22.7 us -> 24.4 us  [exchange_in(): lax.all_to_all(parts, ('seq', 'res'), 0, 0, axis_index_groups=groups, til...]
  transfers between devices with their start and end apart: 9 -> 9, of which waited for: 6 -> 6; matrix products, arithmetic and copies ran while one was open for 1% -> 1% of each run, Pallas kernels for 32% -> 31%
where the time goes in v5:
time: 162 us; the launch traced here: 161 us
  starting transfers between devices  68.1 us (42%)
  Pallas kernels  57.5 us (35%)
  waiting for transfers between devices  29.5 us (18%)
  local copies, waits for them, and re-layouts  5.13 us (3%)
    all_to_all x4, starting transfers between devices, exchange(): return lax.all_to_all(parts, axis, 0, 0, tiled=True)  41.6 us
    all_to_all x3, starting transfers between devices, exchange_in(): lax.all_to_all(parts, ('seq', 'res'), 0, 0, axis_index_groups=groups, til...  24.4 us
    all_to_all x3, waiting for transfers between devices, exchange_in(): lax.all_to_all(parts, ('seq', 'res'), 0, 0, axis_index_groups=groups, til...  23.5 us
    pallas_call x1, Pallas kernels, weight(): pl.pallas_call(functools.partial(weight_kernel, inv_count), grid=(residue...  12 us
    pallas_call x2, Pallas kernels, pair_part(): pl.pallas_call(pair_kernel, grid=(end - begin,), in_specs=[pl.BlockSpec((...  9.93 us
    pallas_call x1, Pallas kernels, grad_outer(): pl.pallas_call(functools.partial(grad_outer_kernel, parts), in_specs=[who...  9.89 us
    pallas_call x1, Pallas kernels, left(): pl.pallas_call(functools.partial(left_kernel, inv_count, parts), in_specs...  9.29 us
    pallas_call x1, Pallas kernels, right(): pl.pallas_call(functools.partial(right_kernel, inv_count, parts), in_spec...  8.58 us
  transfers between devices with their start and end apart: 9, of which 6 were waited for; matrix products, arithmetic and copies ran while one was open for 1% of the time, Pallas kernels for 31%

profile of v5, /device:TPU:1, one launch (start us, length us, event | category | flops | bytes accessed | tf_op | source)
XLA Modules:
  0.0 161.2 jit_solution(18204617169104835277)
XLA Ops:
  0.6 1.9 %before.1 = (bf16[32,128]{1,0:T(8,128)(2,1)}, bf16[144,256]{1,0:T(8,128)(2,1)}) custom-call(bf16[2,64,256]{2,1,0:T(8,128)(2,1)} %x_ref.3, bf16[64,256]{1,0:T(8,128)(2,1)} %bitcast.4), custom_call_target="tpu_custom_call" | custom-call | tf_op jit(solution)/shard_map/before/pallas_call | solution.py:73
  2.5 1.5 collective-permute-start
  4.0 1.4 broadcast_in_dim.6
  5.4 16.6 %all-to-all-start = ((bf16[16,32,128]{2,1,0:T(8,128)(2,1)}), bf16[16,32,128]{2,1,0:T(8,128)(2,1)S(1)}, u32[]{:S(2)}, u32[]{:S(2)}) async-start(bf16[16,32,128]{2,1,0:T(8,128)(2,1)} %broadcast_in_dim.6), calls=%async_computation | async-start | bytes 262144 | tf_op jit(solution)/shard_map/all_to_all | solution.py:552
  22.0 9.9 %grad_outer.1 = (bf16[2048,4096]{1,0:T(8,128)(2,1)}, bf16[1024,128]{1,0:T(8,128)(2,1)}) custom-call(bf16[1024,128]{1,0:T(8,128)(2,1)} %given_ref.1, bf16[64,128,128]{2,1,0:T(8,128)(2,1)} %cot_ref.3), custom_call_target="tpu_custom_call" | custom-call | flops 8000000000 | bytes 4000000 | tf_op jit(solution)/shard_map/grad_outer/pallas_call | solution.py:125
  31.9 0.0 collective-permute-done.moved_ref
  31.9 0.0 copy-start.13
  32.0 1.4 all-to-all-done.recv_ref
  33.3 0.7 broadcast_in_dim.7
  34.1 10.7 %all-to-all-start.1 = ((bf16[32,32,128]{2,1,0:T(8,128)(2,1)}), bf16[32,32,128]{2,1,0:T(8,128)(2,1)S(1)}, u32[]{:S(2)}, u32[]{:S(2)}) async-start(bf16[32,32,128]{2,1,0:T(8,128)(2,1)} %broadcast_in_dim.7), calls=%async_computation.1 | async-start | bytes 524288 | tf_op jit(solution)/shard_map/all_to_all | solution.py:552
  44.8 0.0 copy-done.12
  44.8 8.6 %right.1 = bf16[32,32,128]{2,1,0:T(8,128)(2,1)} custom-call(s32[1]{0:T(128)} %bitcast.1.mine_ref, s32[16,32]{1,0:T(8,128)} %constant.8.clone.slots_ref, bf16[16,32,128]{2,1,0:T(8,128)(2,1)} %copy-done.12, bf16[2048,4096]{1,0:T(8,128)(2,1)} %get-tuple-element.19.grad_ref), custom_call_target="tpu_custom_call" | custom-call | flops 8000000000 | bytes 4000000 | tf_op jit(solution)/shard_map/right/pallas_call | solution.py:176
  53.4 0.0 copy-done.13
  53.4 2.7 %all-to-all-done.1.recv_ref = bf16[32,32,128]{2,1,0:T(8,128)(2,1)S(1)} async-done(((bf16[32,32,128]{2,1,0:T(8,128)(2,1)}), bf16[32,32,128]{2,1,0:T(8,128)(2,1)S(1)}, u32[]{:S(2)}, u32[]{:S(2)}) %all-to-all-start.1) | async-done | bytes 262176 | tf_op jit(solution)/shard_map/all_to_all | solution.py:552
  56.0 5.0 %all-to-all-start.3 = ((bf16[32,32,128]{2,1,0:T(8,128)(2,1)}), bf16[32,32,128]{2,1,0:T(8,128)(2,1)S(1)}, u32[]{:S(2)}, u32[]{:S(2)}) async-start(bf16[32,32,128]{2,1,0:T(8,128)(2,1)} %right.1), calls=%async_computation.3 | async-start | bytes 524288 | tf_op jit(solution)/shard_map/all_to_all | solution.py:552
  61.1 0.0 copy-done.11
  61.1 9.3 %left.1 = (bf16[1024,128]{1,0:T(8,128)(2,1)}, bf16[16,32,128]{2,1,0:T(8,128)(2,1)}) custom-call(s32[1]{0:T(128)} %bitcast.1.mine_ref, s32[16,32]{1,0:T(8,128)} %constant.8.clone.slots_ref, bf16[32,32,128]{2,1,0:T(8,128)(2,1)} %copy-done.11, bf16[2048,4096]{1,0:T(8,128)(2,1)} %get-tuple-element.19.grad_ref), custom_call_target="tpu_custom_call" | custom-call | flops 8000000000 | bytes 4000000 | tf_op jit(solution)/shard_map/left/pallas_call | solution.py:237
  70.4 2.0 %all-to-all-done.3.in_ref = bf16[32,32,128]{2,1,0:T(8,128)(2,1)S(1)} async-done(((bf16[32,32,128]{2,1,0:T(8,128)(2,1)}), bf16[32,32,128]{2,1,0:T(8,128)(2,1)S(1)}, u32[]{:S(2)}, u32[]{:S(2)}) %all-to-all-start.3) | async-done | bytes 262176 | tf_op jit(solution)/shard_map/all_to_all | solution.py:552
  72.4 9.2 %all-to-all-start.2 = ((bf16[16,32,128]{2,1,0:T(8,128)(2,1)}), bf16[16,32,128]{2,1,0:T(8,128)(2,1)S(1)}, u32[]{:S(2)}, u32[]{:S(2)}) async-start(bf16[16,32,128]{2,1,0:T(8,128)(2,1)} %get-tuple-element.23), calls=%async_computation.2 | async-start | bytes 262144 | tf_op jit(solution)/shard_map/all_to_all | solution.py:552
  81.6 12.0 %weight.1 = (bf16[32,32,128]{2,1,0:T(8,128)(2,1)}, bf16[2048,128]{1,0:T(8,128)(2,1)}) custom-call(bf16[16,32,128]{2,1,0:T(8,128)(2,1)} %copy-done.12, bf16[1024,128]{1,0:T(8,128)(2,1)} %get-tuple-element.20.rt_ref, bf16[64,128,128]{2,1,0:T(8,128)(2,1)} %cot_ref.3), custom_call_target="tpu_custom_call" | custom-call | flops 16000000000 | bytes 4000000 | tf_op jit(solution)/shard_map/weight/pallas_call | solution.py:319
  93.6 0.1 total.1.right_ref.in_ref
  93.7 0.0 copy-start.4
  93.7 0.6 copy-done.4
  94.3 0.0 all-to-all-done.2.left_ref
  94.3 0.7 copy-done.1
  94.9 2.1 %payload.1.behind_ref = bf16[32,40,128]{2,1,0:T(8,128)(2,1)} custom-call(bf16[16,32,128]{2,1,0:T(8,128)(2,1)} %copy-done.1, f32[32,128]{1,0:T(8,128)} %copy-done.4, bf16[144,256]{1,0:T(8,128)(2,1)} %get-tuple-element.18.normed_ref, bf16[144,256]{1,0:T(8,128)(2,1)} %copy-done.13, bf16[32,32,128]{2,1,0:T(8,128)(2,1)} %get-tuple-element.24.wo_ref), custom_call_target="tpu_custom_call" | custom-call | tf_op jit(solution)/shard_map/payload/pallas_call | solution.py:428
  97.0 7.7 %all-to-all-start.4 = ((bf16[32,40,128]{2,1,0:T(8,128)(2,1)}), bf16[32,40,128]{2,1,0:T(8,128)(2,1)S(1)}, u32[]{:S(2)}, u32[]{:S(2)}) async-start(bf16[32,40,128]{2,1,0:T(8,128)(2,1)} %payload.1.behind_ref), calls=%async_computation.4 | async-start | bytes 655360 | tf_op jit(solution)/shard_map/all_to_all | solution.py:556
  104.7 0.0 copy-start
  104.7 1.0 copy-done
  105.7 0.7 copy-done.5
  106.5 0.7 collective-permute-start.1
  107.1 0.0 collective-permute-done.1.behind_ref.right_ref
  107.1 10.4 %all-to-all-done.4.in_ref = bf16[32,40,128]{2,1,0:T(8,128)(2,1)S(1)} async-done(((bf16[32,40,128]{2,1,0:T(8,128)(2,1)}), bf16[32,40,128]{2,1,0:T(8,128)(2,1)S(1)}, u32[]{:S(2)}, u32[]{:S(2)}) %all-to-all-start.4) | async-done | bytes 327712 | tf_op jit(solution)/shard_map/all_to_all | solution.py:556
  117.6 0.7 total_copies.2.refs_0_
  118.3 9.7 %all-to-all-start.5 = ((bf16[16,40,128]{2,1,0:T(8,128)(2,1)}), bf16[16,40,128]{2,1,0:T(8,128)(2,1)S(1)}, u32[]{:S(2)}, u32[]{:S(2)}) async-start(bf16[16,40,128]{2,1,0:T(8,128)(2,1)} %total_copies.2.refs_0_), calls=%async_computation.5 | async-start | bytes 327680 | tf_op jit(solution)/shard_map/all_to_all | solution.py:556
  128.0 0.0 copy-start.3
  128.0 0.0 copy-start.6
  128.0 5.0 %pair_part.2 = (bf16[64,128,128]{2,1,0:T(8,128)(2,1)}, f32[8,128]{1,0:T(8,128)S(1)}) custom-call(bf16[2048,128]{1,0:T(8,128)(2,1)S(1)} %copy-done.9, bf16[1024,128]{1,0:T(8,128)(2,1)S(1)} %copy-done.10, bf16[1024,128]{1,0:T(8,128)(2,1)S(1)} %copy-done.8, f32[1,128]{1,0:T(1,128)S(1)} %bitcast.6, bf16[16,40,128]{2,1,0:T(8,128)(2,1)} %total_copies.2.refs_0_), custom_call_target="tpu_custom_call" | custom-call | flops 6000000000 | bytes 4000000 | tf_op jit(solution)/shard_map/pair_part/pallas_call | solution.py:374
  133.0 4.6 %all-to-all-done.5.in_ref = bf16[16,40,128]{2,1,0:T(8,128)(2,1)S(1)} async-done(((bf16[16,40,128]{2,1,0:T(8,128)(2,1)}), bf16[16,40,128]{2,1,0:T(8,128)(2,1)S(1)}, u32[]{:S(2)}, u32[]{:S(2)}) %all-to-all-start.5) | async-done | bytes 163872 | tf_op jit(solution)/shard_map/all_to_all | solution.py:556
  137.6 0.8 total_copies.3.refs_0_.behind_ref
  138.4 7.0 %all-to-all-start.6 = ((bf16[32,40,128]{2,1,0:T(8,128)(2,1)}), bf16[32,40,128]{2,1,0:T(8,128)(2,1)S(1)}, u32[]{:S(2)}, u32[]{:S(2)}) async-start(bf16[32,40,128]{2,1,0:T(8,128)(2,1)} %total_copies.3.refs_0_.behind_ref), calls=%async_computation.6 | async-start | bytes 655360 | tf_op jit(solution)/shard_map/all_to_all | solution.py:556
  145.4 0.0 copy-done.2
  145.4 0.0 copy-done.3
  145.4 0.0 copy-done.6
  145.4 1.0 align.1
  146.4 5.0 %pair_part.3 = (bf16[64,128,128]{2,1,0:T(8,128)(2,1)}, f32[8,128]{1,0:T(8,128)}) custom-call(bf16[2048,128]{1,0:T(8,128)(2,1)S(1)} %copy-done.9, bf16[1024,128]{1,0:T(8,128)(2,1)S(1)} %copy-done.10, bf16[1024,128]{1,0:T(8,128)(2,1)S(1)} %copy-done.8, f32[1,128]{1,0:T(1,128)S(1)} %bitcast.7, ...), custom_call_target="tpu_custom_call", output_to_operand_aliasing={{0}: (5, {})} | custom-call | flops 6000000000 | bytes 4000000 | tf_op jit(solution)/shard_map/pair_part/pallas_call | solution.py:374
  151.4 8.5 %all-to-all-done.6.in_ref = bf16[32,40,128]{2,1,0:T(8,128)(2,1)S(1)} async-done(((bf16[32,40,128]{2,1,0:T(8,128)(2,1)}), bf16[32,40,128]{2,1,0:T(8,128)(2,1)S(1)}, u32[]{:S(2)}, u32[]{:S(2)}) %all-to-all-start.6) | async-done | bytes 327712 | tf_op jit(solution)/shard_map/all_to_all | solution.py:556
  159.9 1.3 last.1
  (16 shorter events, 0.0 us)
Async XLA Ops:
  2.5 29.4 %collective-permute-start = (bf16[144,256]{1,0:T(8,128)(2,1)}, bf16[144,256]{1,0:T(8,128)(2,1)S(1)}, u32[]{:S(2)}, u32[]{:S(2)}) collective-permute-start(bf16[144,256]{1,0:T(8,128)(2,1)} %get-tuple-element.18.normed_ref), channel_id=1, source_target_pairs={{0,0},{1,1},{448,2},{449,3},{480,4},{481,5},{384,6},{385,7},{32,8}... | collective-permute-start | bytes 221192 | tf_op jit(solution)/shard_map/ppermute | solution.py:615
  5.4 28.0 %all-to-all-start = ((bf16[16,32,128]{2,1,0:T(8,128)(2,1)}), bf16[16,32,128]{2,1,0:T(8,128)(2,1)S(1)}, u32[]{:S(2)}, u32[]{:S(2)}) async-start(bf16[16,32,128]{2,1,0:T(8,128)(2,1)} %broadcast_in_dim.6), calls=%async_computation | async-start | bytes 262144 | tf_op jit(solution)/shard_map/all_to_all | solution.py:552
  31.9 21.4 %copy-start.13 = (bf16[144,256]{1,0:T(8,128)(2,1)}, bf16[144,256]{1,0:T(8,128)(2,1)S(1)}, u32[]{:S(2)}) copy-start(bf16[144,256]{1,0:T(8,128)(2,1)S(1)} %collective-permute-done.moved_ref) | copy-start | bytes 221188
  33.3 11.4 %copy-start.12 = (bf16[16,32,128]{2,1,0:T(8,128)(2,1)}, bf16[16,32,128]{2,1,0:T(8,128)(2,1)S(1)}, u32[]{:S(2)}) copy-start(bf16[16,32,128]{2,1,0:T(8,128)(2,1)S(1)} %all-to-all-done.recv_ref) | copy-start | bytes 393220
  34.1 21.9 %all-to-all-start.1 = ((bf16[32,32,128]{2,1,0:T(8,128)(2,1)}), bf16[32,32,128]{2,1,0:T(8,128)(2,1)S(1)}, u32[]{:S(2)}, u32[]{:S(2)}) async-start(bf16[32,32,128]{2,1,0:T(8,128)(2,1)} %broadcast_in_dim.7), calls=%async_computation.1 | async-start | bytes 524288 | tf_op jit(solution)/shard_map/all_to_all | solution.py:552
  56.0 5.1 %copy-start.11 = (bf16[32,32,128]{2,1,0:T(8,128)(2,1)}, bf16[32,32,128]{2,1,0:T(8,128)(2,1)S(1)}, u32[]{:S(2)}) copy-start(bf16[32,32,128]{2,1,0:T(8,128)(2,1)S(1)} %all-to-all-done.1.recv_ref) | copy-start | bytes 786436
  56.0 16.3 %all-to-all-start.3 = ((bf16[32,32,128]{2,1,0:T(8,128)(2,1)}), bf16[32,32,128]{2,1,0:T(8,128)(2,1)S(1)}, u32[]{:S(2)}, u32[]{:S(2)}) async-start(bf16[32,32,128]{2,1,0:T(8,128)(2,1)} %right.1), calls=%async_computation.3 | async-start | bytes 524288 | tf_op jit(solution)/shard_map/all_to_all | solution.py:552
  72.4 21.9 %all-to-all-start.2 = ((bf16[16,32,128]{2,1,0:T(8,128)(2,1)}), bf16[16,32,128]{2,1,0:T(8,128)(2,1)S(1)}, u32[]{:S(2)}, u32[]{:S(2)}) async-start(bf16[16,32,128]{2,1,0:T(8,128)(2,1)} %get-tuple-element.23), calls=%async_computation.2 | async-start | bytes 262144 | tf_op jit(solution)/shard_map/all_to_all | solution.py:552
  93.6 34.4 %copy-start.7 = (f32[128]{0:T(128)S(1)}, f32[128]{0:T(128)}, u32[]{:S(2)}) copy-start(f32[128]{0:T(128)} %param.9) | copy-start | bytes 1540
  93.6 34.4 %copy-start.8 = (bf16[1024,128]{1,0:T(8,128)(2,1)S(1)}, bf16[1024,128]{1,0:T(8,128)(2,1)}, u32[]{:S(2)}) copy-start(bf16[1024,128]{1,0:T(8,128)(2,1)} %get-tuple-element.20.rt_ref) | copy-start | bytes 786436
  93.6 34.4 %copy-start.9 = (bf16[2048,128]{1,0:T(8,128)(2,1)S(1)}, bf16[2048,128]{1,0:T(8,128)(2,1)}, u32[]{:S(2)}) copy-start(bf16[2048,128]{1,0:T(8,128)(2,1)} %get-tuple-element.21.rows_ref) | copy-start | bytes 1572868
  93.6 34.4 %copy-start.10 = (bf16[1024,128]{1,0:T(8,128)(2,1)S(1)}, bf16[1024,128]{1,0:T(8,128)(2,1)}, u32[]{:S(2)}) copy-start(bf16[1024,128]{1,0:T(8,128)(2,1)} %get-tuple-element.22.w_ref) | copy-start | bytes 786436
  93.7 0.6 copy-start.4
  94.3 0.7 copy-start.1
  97.0 20.5 %all-to-all-start.4 = ((bf16[32,40,128]{2,1,0:T(8,128)(2,1)}), bf16[32,40,128]{2,1,0:T(8,128)(2,1)S(1)}, u32[]{:S(2)}, u32[]{:S(2)}) async-start(bf16[32,40,128]{2,1,0:T(8,128)(2,1)} %payload.1.behind_ref), calls=%async_computation.4 | async-start | bytes 655360 | tf_op jit(solution)/shard_map/all_to_all | solution.py:556
  104.7 1.0 copy-start
  105.7 0.7 copy-start.5
  106.5 0.7 collective-permute-start.1
  118.3 19.3 %all-to-all-start.5 = ((bf16[16,40,128]{2,1,0:T(8,128)(2,1)}), bf16[16,40,128]{2,1,0:T(8,128)(2,1)S(1)}, u32[]{:S(2)}, u32[]{:S(2)}) async-start(bf16[16,40,128]{2,1,0:T(8,128)(2,1)} %total_copies.2.refs_0_), calls=%async_computation.5 | async-start | bytes 327680 | tf_op jit(solution)/shard_map/all_to_all | solution.py:556
  128.0 17.4 %copy-start.2 = (bf16[16,32,128]{2,1,0:T(8,128)(2,1)S(1)}, bf16[16,32,128]{2,1,0:T(8,128)(2,1)}, u32[]{:S(2)}) copy-start(bf16[16,32,128]{2,1,0:T(8,128)(2,1)} %copy-done.1) | copy-start | bytes 393220
  128.0 17.4 %copy-start.3 = (bf16[2,64,256]{2,1,0:T(8,128)(2,1)S(1)}, bf16[2,64,256]{2,1,0:T(8,128)(2,1)}, u32[]{:S(2)}) copy-start(bf16[2,64,256]{2,1,0:T(8,128)(2,1)} %x_ref.3) | copy-start | bytes 196612
  128.0 17.4 %copy-start.6 = (bf16[256,64]{0,1:T(8,128)(2,1)S(1)}, bf16[256,64]{0,1:T(8,128)(2,1)}, u32[]{:S(2)}) copy-start(bf16[256,64]{0,1:T(8,128)(2,1)} %param.7) | copy-start | bytes 98308
  138.4 21.5 %all-to-all-start.6 = ((bf16[32,40,128]{2,1,0:T(8,128)(2,1)}), bf16[32,40,128]{2,1,0:T(8,128)(2,1)S(1)}, u32[]{:S(2)}, u32[]{:S(2)}) async-start(bf16[32,40,128]{2,1,0:T(8,128)(2,1)} %total_copies.3.refs_0_.behind_ref), calls=%async_computation.6 | async-start | bytes 655360 | tf_op jit(solution)/shard_map/all_to_all | solution.py:556
